TPU v7x, 32 devices: a whole 2x2x4 slice. The times are simulated.
32 devices in a mesh: dp: 8 (over z, x), mp: 4 (over y, core).
Axes of the slice: x: 2, y: 2, z: 4, core: 2. Of those that a mesh axis runs over, the one named last changes fastest.
Arguments:
- block_input: bfloat16 [16384, 768], P(('dp', 'mp')), may hold values from -6 to 6
- cotangent: bfloat16 [16384, 768], P(('dp', 'mp')), may hold values from -5.2 to 5.2
- lengths: int32 [256], P('dp'), may hold values from 3 to 64, as said below
- attn_input: float32 [768, 3, 768], P('dp', None, 'mp')
- attn_input_first: float32 [768, 3, 768], P('dp', None, 'mp'), may hold values from -0.005859375 to 0.005859375
- attn_input_second: float32 [768, 3, 768], P('dp', None, 'mp'), may hold values from 1.4110135e-07 to 5.644054e-07
- attn_output: float32 [768, 768], P('dp', 'mp'), may hold values from -0.875 to 0.875
- attn_output_first: float32 [768, 768], P('dp', 'mp'), may hold values from -0.005859375 to 0.005859375
- attn_output_second: float32 [768, 768], P('dp', 'mp'), may hold values from 1.4110135e-07 to 5.644054e-07
- mlp_up: float32 [768, 3072], P('dp', 'mp')
- mlp_up_first: float32 [768, 3072], P('dp', 'mp'), may hold values from -0.0017089844 to 0.0017089844
- mlp_up_second: float32 [768, 3072], P('dp', 'mp'), may hold values from 1.4110136e-08 to 5.6440545e-08
- mlp_down: float32 [768, 3072], P('dp', 'mp'), may hold values from -0.109375 to 0.109375
- mlp_down_first: float32 [768, 3072], P('dp', 'mp'), may hold values from -0.005859375 to 0.005859375
- mlp_down_second: float32 [768, 3072], P('dp', 'mp'), may hold values from 1.4110135e-07 to 5.644054e-07
- norm_params: float32 [4, 768], replicated, may hold values from -1.2 to 2.1
- norm_first: float32 [4, 768], P(None, ('dp', 'mp')), may hold values from -0.005859375 to 0.005859375
- norm_second: float32 [4, 768], P(None, ('dp', 'mp')), may hold values from 1.4110135e-07 to 5.644054e-07
- bias_params: float32 [8, 768], replicated, may hold values from -4 to 4
- bias_first: float32 [8, 768], P(None, ('dp', 'mp')), may hold values from -0.005859375 to 0.005859375
- bias_second: float32 [8, 768], P(None, ('dp', 'mp')), may hold values from 1.4110135e-07 to 5.644054e-07
Outputs:
- block_output: bfloat16 [16384, 768], P(('dp', 'mp'))
- input_grad: float32 [16384, 768], P(('dp', 'mp'))
- grad_norm: float32 [], replicated
- attn_input_grad: float32 [768, 3, 768], P('dp', None, 'mp')
- attn_input_new: float32 [768, 3, 768], P('dp', None, 'mp')
- attn_input_first_new: float32 [768, 3, 768], P('dp', None, 'mp')
- attn_input_second_new: float32 [768, 3, 768], P('dp', None, 'mp')
- attn_input_copy: bfloat16 [768, 3, 768], P('dp', None, 'mp')
- attn_output_grad: float32 [768, 768], P('dp', 'mp')
- attn_output_new: float32 [768, 768], P('dp', 'mp')
- attn_output_first_new: float32 [768, 768], P('dp', 'mp')
- attn_output_second_new: float32 [768, 768], P('dp', 'mp')
- attn_output_copy: bfloat16 [768, 768], P('dp', 'mp')
- mlp_up_grad: float32 [768, 3072], P('dp', 'mp')
- mlp_up_new: float32 [768, 3072], P('dp', 'mp')
- mlp_up_first_new: float32 [768, 3072], P('dp', 'mp')
- mlp_up_second_new: float32 [768, 3072], P('dp', 'mp')
- mlp_up_copy: bfloat16 [768, 3072], P('dp', 'mp')
- mlp_down_grad: float32 [768, 3072], P('dp', 'mp')
- mlp_down_new: float32 [768, 3072], P('dp', 'mp')
- mlp_down_first_new: float32 [768, 3072], P('dp', 'mp')
- mlp_down_second_new: float32 [768, 3072], P('dp', 'mp')
- mlp_down_copy: bfloat16 [768, 3072], P('dp', 'mp')
- norm_grad: float32 [4, 768], P(None, ('dp', 'mp'))
- norm_new: float32 [4, 768], P(None, ('dp', 'mp'))
- norm_first_new: float32 [4, 768], P(None, ('dp', 'mp'))
- norm_second_new: float32 [4, 768], P(None, ('dp', 'mp'))
- bias_grad: float32 [8, 768], P(None, ('dp', 'mp'))
- bias_new: float32 [8, 768], P(None, ('dp', 'mp'))
- bias_first_new: float32 [8, 768], P(None, ('dp', 'mp'))
- bias_second_new: float32 [8, 768], P(None, ('dp', 'mp'))
Inputs may be any that keep to these rules, and one draw needn't show every extreme that they name: `lengths`: mostly short; in every aligned block of 8 * 4 captions one caption has length 64.
All inputs are finite; a program needn't handle non-finite values.
Results may differ from a plain program's by a relative error of at most 0.018.
Values may be sent and summed in bfloat16 or wider, within the bound.
No kernel may reach another device: no remote copies, remote signals or barrier semaphores. Data moves between devices by JAX's collectives and lax.ppermute only.
A program may use at most 128 MiB of HBM per device.

v0:
```python
import jax
import jax.numpy as jnp
from jax import lax
from jax.sharding import PartitionSpec as P

HEAD = 64
STEP = 10


norm_eps = 1e-06
beta_first = 0.5
beta_second = 0.5
adam_eps = 1e-08
matrix_rate = 0.03
small_rate = 0.3
matrix_decay = 0.01
clip_limit = 1.0
masked_score = -1e30


def layer_norm(rows, gain, shift):
    center = jnp.mean(rows, axis=1, keepdims=True)
    centered = rows - center
    spread = jnp.mean(centered * centered, axis=1, keepdims=True)
    inverse = lax.rsqrt(spread + norm_eps)
    normed = centered * inverse
    return (normed * gain + shift, normed, inverse)


def norm_backward(grad_rows, normed, inverse, gain):
    scaled = grad_rows * gain
    back = inverse * (
        scaled
        - jnp.mean(scaled, axis=1, keepdims=True)
        - normed * jnp.mean(scaled * normed, axis=1, keepdims=True)
    )
    return (back, jnp.sum(grad_rows * normed, axis=0), jnp.sum(grad_rows, axis=0))


def gelu_tanh(values):
    return jax.nn.gelu(values, approximate=True)


def contract_rows(left, right):
    return lax.dot_general(
        left, right, (((0,), (0,)), ((), ())), preferred_element_type=jnp.float32
    )


def contract_cols(left, right):
    return lax.dot_general(
        left, right, (((1,), (1,)), ((), ())), preferred_element_type=jnp.float32
    )


def masked_scores(query, keys_all, valid, scale):
    raw = jnp.einsum("cqhd,ckhd->chqk", query, keys_all, preferred_element_type=jnp.float32) * scale
    return jnp.where(valid[:, None, None, :], raw, masked_score)


def adam_step(weight, first, second, grad, rate, decay):
    first_new = beta_first * first + (1.0 - beta_first) * grad
    second_new = beta_second * second + (1.0 - beta_second) * grad * grad
    first_hat = first_new / (1.0 - beta_first**STEP)
    second_hat = second_new / (1.0 - beta_second**STEP)
    weight_new = weight - rate * (first_hat / (jnp.sqrt(second_hat) + adam_eps) + decay * weight)
    return (weight_new, first_new, second_new)


def body(
    block_input,
    cotangent,
    lengths,
    attn_input,
    attn_input_first,
    attn_input_second,
    attn_output,
    attn_output_first,
    attn_output_second,
    mlp_up,
    mlp_up_first,
    mlp_up_second,
    mlp_down,
    mlp_down_first,
    mlp_down_second,
    norm_params,
    norm_first,
    norm_second,
    bias_params,
    bias_first,
    bias_second,
):
    width = norm_params.shape[1]
    units = bias_params.shape[0] - 4
    head_cols = attn_input.shape[2]
    hidden_cols = mlp_up.shape[1]
    rank = lax.axis_index("mp")
    groups = lax.axis_size("mp")
    captions = lengths.shape[0]
    length = block_input.shape[0] * groups // captions
    heads_here = head_cols // HEAD
    scale = HEAD ** (-0.5)
    full_input, full_output, full_up, full_down = (
        lax.all_gather(attn_input.astype(jnp.bfloat16), "dp", axis=0, tiled=True),
        lax.all_gather(attn_output.astype(jnp.bfloat16), "dp", axis=0, tiled=True),
        lax.all_gather(mlp_up.astype(jnp.bfloat16), "dp", axis=0, tiled=True),
        lax.all_gather(mlp_down.astype(jnp.bfloat16), "dp", axis=0, tiled=True),
    )
    joined_weight = full_input.reshape(width, 3 * head_cols)
    positions = lax.broadcasted_iota(jnp.int32, (captions, length), 1)
    valid = positions < lengths[:, None]
    own_caps = captions // groups
    row_valid = (
        lax.dynamic_slice_in_dim(valid, rank * own_caps, own_caps, 0)
        .reshape(-1, 1)
        .astype(jnp.float32)
    )

    def split(tensor):
        return tensor.reshape(captions, length, heads_here, HEAD)

    rows = block_input.astype(jnp.float32)
    normed_one, unit_one, inverse_one = layer_norm(rows, norm_params[0], norm_params[1])
    group_one = lax.all_gather(normed_one.astype(jnp.bfloat16), "mp", axis=0, tiled=True)
    joined = jnp.dot(group_one, joined_weight, preferred_element_type=jnp.float32)
    query_bias = lax.dynamic_slice_in_dim(bias_params[units], rank * head_cols, head_cols, 0)
    value_bias = lax.dynamic_slice_in_dim(bias_params[units + 1], rank * head_cols, head_cols, 0)
    query = (joined[:, :head_cols] + query_bias).astype(jnp.bfloat16)
    keys_all = joined[:, head_cols : 2 * head_cols].astype(jnp.bfloat16)
    values = (joined[:, 2 * head_cols :] + value_bias).astype(jnp.bfloat16)
    scores = masked_scores(split(query), split(keys_all), valid, scale)
    top = jnp.max(scores, axis=-1, keepdims=True)
    expo = jnp.exp(scores - top)
    total = jnp.sum(expo, axis=-1, keepdims=True)
    probs = (expo / total).astype(jnp.bfloat16)
    log_total = top + jnp.log(total)
    attended = (
        jnp.einsum("chqk,ckhd->cqhd", probs, split(values), preferred_element_type=jnp.float32)
        .reshape(-1, head_cols)
        .astype(jnp.bfloat16)
    )
    branch = lax.psum_scatter(
        contract_cols(attended, full_output).astype(jnp.bfloat16),
        "mp",
        scatter_dimension=0,
        tiled=True,
    ).astype(jnp.float32)
    middle = rows + branch + bias_params[units + 2]
    normed_two, unit_two, inverse_two = layer_norm(middle, norm_params[2], norm_params[3])
    group_two = lax.all_gather(normed_two.astype(jnp.bfloat16), "mp", axis=0, tiled=True)
    up_bias = lax.dynamic_slice_in_dim(
        bias_params[:units].reshape(-1), rank * hidden_cols, hidden_cols, 0
    )
    expanded = jnp.dot(group_two, full_up, preferred_element_type=jnp.float32) + up_bias
    activated, gelu_pull = jax.vjp(gelu_tanh, expanded)
    hidden = activated.astype(jnp.bfloat16)
    branch_two = lax.psum_scatter(
        contract_cols(hidden, full_down).astype(jnp.bfloat16), "mp", scatter_dimension=0, tiled=True
    ).astype(jnp.float32)
    block_output = (middle + branch_two + bias_params[units + 3]).astype(jnp.bfloat16)
    grad_out = cotangent.astype(jnp.float32) * row_valid
    group_grad = lax.all_gather(grad_out.astype(jnp.bfloat16), "mp", axis=0, tiled=True)
    down_grad = contract_rows(group_grad, hidden)
    hidden_grad = jnp.dot(group_grad, full_down, preferred_element_type=jnp.float32)
    expanded_grad = gelu_pull(hidden_grad)[0].astype(jnp.bfloat16)
    up_grad = contract_rows(group_two, expanded_grad)
    up_bias_grad = jnp.sum(expanded_grad.astype(jnp.float32), axis=0)
    two_grad = lax.psum_scatter(
        contract_cols(expanded_grad, full_up).astype(jnp.bfloat16),
        "mp",
        scatter_dimension=0,
        tiled=True,
    ).astype(jnp.float32)
    middle_norm_grad, gain_two_grad, shift_two_grad = norm_backward(
        two_grad, unit_two, inverse_two, norm_params[2]
    )
    middle_grad = grad_out + middle_norm_grad
    group_middle = lax.all_gather(middle_grad.astype(jnp.bfloat16), "mp", axis=0, tiled=True)
    output_grad = contract_rows(group_middle, attended)
    attended_grad = jnp.dot(group_middle, full_output, preferred_element_type=jnp.float32).astype(
        jnp.bfloat16
    )
    again = masked_scores(split(query), split(keys_all), valid, scale)
    weights_full = jnp.exp(again - log_total)
    probs_grad = jnp.einsum(
        "cqhd,ckhd->chqk", split(attended_grad), split(values), preferred_element_type=jnp.float32
    )
    values_grad = (
        jnp.einsum(
            "chqk,cqhd->ckhd",
            weights_full.astype(jnp.bfloat16),
            split(attended_grad),
            preferred_element_type=jnp.float32,
        )
        .reshape(-1, head_cols)
        .astype(jnp.bfloat16)
    )
    shared = jnp.sum(weights_full * probs_grad, axis=-1, keepdims=True)
    scores_grad = (weights_full * (probs_grad - shared)).astype(jnp.bfloat16)
    query_grad = (
        (
            jnp.einsum(
                "chqk,ckhd->cqhd", scores_grad, split(keys_all), preferred_element_type=jnp.float32
            )
            * scale
        )
        .reshape(-1, head_cols)
        .astype(jnp.bfloat16)
    )
    keys_grad = (
        (
            jnp.einsum(
                "chqk,cqhd->ckhd", scores_grad, split(query), preferred_element_type=jnp.float32
            )
            * scale
        )
        .reshape(-1, head_cols)
        .astype(jnp.bfloat16)
    )
    joined_grad = jnp.concatenate([query_grad, keys_grad, values_grad], axis=1)
    input_weight_grad = contract_rows(group_one, joined_grad).reshape(width, 3, head_cols)
    query_bias_grad = jnp.sum(query_grad.astype(jnp.float32), axis=0)
    value_bias_grad = jnp.sum(values_grad.astype(jnp.float32), axis=0)
    one_grad = lax.psum_scatter(
        contract_cols(joined_grad, joined_weight).astype(jnp.bfloat16),
        "mp",
        scatter_dimension=0,
        tiled=True,
    ).astype(jnp.float32)
    rows_norm_grad, gain_one_grad, shift_one_grad = norm_backward(
        one_grad, unit_one, inverse_one, norm_params[0]
    )
    input_grad = middle_grad + rows_norm_grad
    norm_grad_full = jnp.stack([gain_one_grad, shift_one_grad, gain_two_grad, shift_two_grad])
    zero_line = jnp.zeros((width,), jnp.float32)
    up_lines = lax.dynamic_update_slice_in_dim(
        jnp.zeros((units * width,), jnp.float32), up_bias_grad, rank * hidden_cols, 0
    ).reshape(units, width)
    query_line = lax.dynamic_update_slice_in_dim(zero_line, query_bias_grad, rank * head_cols, 0)
    value_line = lax.dynamic_update_slice_in_dim(zero_line, value_bias_grad, rank * head_cols, 0)
    tail_lines = jnp.stack(
        [query_line, value_line, jnp.sum(middle_grad, axis=0), jnp.sum(grad_out, axis=0)]
    )
    bias_grad_full = jnp.concatenate([up_lines, tail_lines], axis=0)
    norm_sum, bias_sum = (
        lax.psum_scatter(norm_grad_full, ("dp", "mp"), scatter_dimension=1, tiled=True),
        lax.psum_scatter(bias_grad_full, ("dp", "mp"), scatter_dimension=1, tiled=True),
    )
    input_sum, output_sum, up_sum, down_sum = (
        lax.psum_scatter(input_weight_grad, "dp", scatter_dimension=0, tiled=True),
        lax.psum_scatter(output_grad, "dp", scatter_dimension=0, tiled=True),
        lax.psum_scatter(up_grad, "dp", scatter_dimension=0, tiled=True),
        lax.psum_scatter(down_grad, "dp", scatter_dimension=0, tiled=True),
    )
    reduced = (input_sum, output_sum, up_sum, down_sum, norm_sum, bias_sum)
    local_squares = jnp.zeros((), jnp.float32)
    for grad in reduced:
        local_squares = local_squares + jnp.sum(grad * grad)
    grad_norm = jnp.sqrt(lax.psum(local_squares, ("dp", "mp")))
    factor = jnp.minimum(1.0, clip_limit / (grad_norm + 1e-06))
    columns = norm_first.shape[1]
    offset = (lax.axis_index("dp") * groups + rank) * columns
    own_norm = lax.dynamic_slice_in_dim(norm_params, offset, columns, 1)
    own_bias = lax.dynamic_slice_in_dim(bias_params, offset, columns, 1)
    results = [block_output, input_grad, grad_norm]
    matrices = (
        (attn_input, attn_input_first, attn_input_second, input_sum),
        (attn_output, attn_output_first, attn_output_second, output_sum),
        (mlp_up, mlp_up_first, mlp_up_second, up_sum),
        (mlp_down, mlp_down_first, mlp_down_second, down_sum),
    )
    for weight, first, second, grad in matrices:
        clipped = grad * factor
        new, first_new, second_new = adam_step(
            weight, first, second, clipped, matrix_rate, matrix_decay
        )
        results += [clipped, new, first_new, second_new, new.astype(jnp.bfloat16)]
    smalls = (
        (own_norm, norm_first, norm_second, norm_sum),
        (own_bias, bias_first, bias_second, bias_sum),
    )
    for weight, first, second, grad in smalls:
        clipped = grad * factor
        new, first_new, second_new = adam_step(weight, first, second, clipped, small_rate, 0.0)
        results += [clipped, new, first_new, second_new]
    return tuple(results)


def solution(mesh):
    return jax.shard_map(
        body,
        mesh=mesh,
        in_specs=(
            P(("dp", "mp"), None),
            P(("dp", "mp"), None),
            P("dp"),
            P("dp", None, "mp"),
            P("dp", None, "mp"),
            P("dp", None, "mp"),
            P("dp", "mp"),
            P("dp", "mp"),
            P("dp", "mp"),
            P("dp", "mp"),
            P("dp", "mp"),
            P("dp", "mp"),
            P("dp", "mp"),
            P("dp", "mp"),
            P("dp", "mp"),
            P(),
            P(None, ("dp", "mp")),
            P(None, ("dp", "mp")),
            P(),
            P(None, ("dp", "mp")),
            P(None, ("dp", "mp")),
        ),
        out_specs=(
            P(("dp", "mp"), None),
            P(("dp", "mp"), None),
            P(),
            P("dp", None, "mp"),
            P("dp", None, "mp"),
            P("dp", None, "mp"),
            P("dp", None, "mp"),
            P("dp", None, "mp"),
            P("dp", "mp"),
            P("dp", "mp"),
            P("dp", "mp"),
            P("dp", "mp"),
            P("dp", "mp"),
            P("dp", "mp"),
            P("dp", "mp"),
            P("dp", "mp"),
            P("dp", "mp"),
            P("dp", "mp"),
            P("dp", "mp"),
            P("dp", "mp"),
            P("dp", "mp"),
            P("dp", "mp"),
            P("dp", "mp"),
            P(None, ("dp", "mp")),
            P(None, ("dp", "mp")),
            P(None, ("dp", "mp")),
            P(None, ("dp", "mp")),
            P(None, ("dp", "mp")),
            P(None, ("dp", "mp")),
            P(None, ("dp", "mp")),
            P(None, ("dp", "mp")),
        ),
        check_vma=False,
    )
```

profile of v0, /device:TPU:0, one launch (start us, length us, event | category | flops | bytes accessed | tf_op | source)
XLA Modules:
  0.0 816.2 jit_solution(9235265508734200853)
XLA Ops:
  13.3 38.9 %all_gather.25 = bf16[768,3,192]{2,1,0:T(4,128)(2,1)S(1)} all-gather(bf16[96,3,192]{2,1,0:T(4,128)(2,1)S(1)} %copy.102), channel_id=1, replica_groups=mesh['dp'=8,'mp'=4] {'dp'}, dimensions={0}, use_global_device_ids=true | all-gather | bytes 995328 | tf_op jit(solution)/shard_map/all_gather | solution.py:104
  54.9 31.2 %all_gather.26 = bf16[768,192]{1,0:T(8,128)(2,1)S(1)} all-gather(bf16[96,192]{1,0:T(8,128)(2,1)S(1)} %convert_element_type.167), channel_id=1, replica_groups=mesh['dp'=8,'mp'=4] {'dp'}, dimensions={0}, use_global_device_ids=true | all-gather | bytes 331776 | tf_op jit(solution)/shard_map/all_gather | solution.py:105
  86.2 4.1 fusion.66
  103.1 3.8 fusion.65
  116.5 35.6 %reduce-scatter.11.cloned.1.call-done = bf16[512,768]{1,0:T(8,128)(2,1)} async-done(((bf16[2048,768]{1,0:T(8,128)(2,1)}), bf16[512,768]{1,0:T(8,128)(2,1)}) %reduce-scatter.11.cloned.1.call-update) | async-done | bytes 786448 | tf_op jit(solution)/shard_map/reduce_scatter | solution.py:142
  159.0 29.0 %all-gather.9.cloned.1.call-done = bf16[2048,768]{1,0:T(8,128)(2,1)} async-done(((bf16[512,768]{1,0:T(8,128)(2,1)}), bf16[2048,768]{1,0:T(8,128)(2,1)}) %all-gather.9.cloned.1.call-update) | async-done | bytes 3145744 | tf_op jit(solution)/shard_map/all_gather | solution.py:150
  188.0 7.5 fusion.67
  195.5 36.9 %all-gather.13.cloned.1.call-done = bf16[768,768]{1,0:T(8,128)(2,1)} async-done(((bf16[96,768]{1,0:T(8,128)(2,1)}), bf16[768,768]{1,0:T(8,128)(2,1)}) %all-gather.13.cloned.1.call-update) | async-done | bytes 1179664 | tf_op jit(solution)/shard_map/all_gather | solution.py:107
  232.4 29.1 %all-gather.15.cloned.1.call-done = bf16[2048,768]{1,0:T(8,128)(2,1)} async-done(((bf16[512,768]{1,0:T(8,128)(2,1)}), bf16[2048,768]{1,0:T(8,128)(2,1)}) %all-gather.15.cloned.1.call-update) | async-done | bytes 3145744 | tf_op jit(solution)/shard_map/all_gather | solution.py:162
  261.5 10.9 %convert_reduce_fusion = (f32[768]{0:T(1024)}, bf16[2048,768]{1,0:T(8,128)(2,1)S(1)}, bf16[2048,768]{1,0:T(8,128)(2,1)}) fusion(f32[2048,768]{1,0:T(8,128)} %fusion.67, f32[768]{0:T(1024)S(1)} %dynamic_slice.20, bf16[2048,768]{1,0:T(8,128)(2,1)} %all-gather.15.cloned.1.call-done, bf16[768,768]{1,0:T(8,128)(2,1)} %all-gather.13.cloned.1.call-done), kind=kOutput, calls=%fused_computation.9 | convolution fusion | flops 2455239936 | bytes 16914432 | tf_op jit(solution)/shard_map/dot_general | solution.py:164
  274.1 4.0 convolution_convert_fusion
  278.2 6.5 convolution_convert_fusion.1
  285.2 31.1 %reduce-scatter.15.cloned.1.call-done = bf16[512,768]{1,0:T(8,128)(2,1)} async-done(((bf16[2048,768]{1,0:T(8,128)(2,1)}), bf16[512,768]{1,0:T(8,128)(2,1)}) %reduce-scatter.15.cloned.1.call-update) | async-done | bytes 786448 | tf_op jit(solution)/shard_map/reduce_scatter | solution.py:168
  320.1 36.5 %reduce-scatter.13.cloned.1.call-done = bf16[512,768]{1,0:T(8,128)(2,1)} async-done(((bf16[2048,768]{1,0:T(8,128)(2,1)}), bf16[512,768]{1,0:T(8,128)(2,1)}) %reduce-scatter.13.cloned.1.call-update) | async-done | bytes 786448 | tf_op jit(solution)/shard_map/reduce_scatter | solution.py:157
  356.7 3.7 fusion.61
  362.6 7.0 fusion.69
  369.6 7.5 fusion.70
  378.0 13.0 %all-gather.17.cloned.1.call-done = bf16[2048,768]{1,0:T(8,128)(2,1)} async-done(((bf16[512,768]{1,0:T(8,128)(2,1)}), bf16[2048,768]{1,0:T(8,128)(2,1)}) %all-gather.17.cloned.1.call-update) | async-done | bytes 3145744 | tf_op jit(solution)/shard_map/all_gather | solution.py:178
  391.0 3.1 convolution_convert_fusion.4
  399.2 3.5 multiply_reduce_fusion
  406.2 3.2 copy.113
  412.2 4.3 fusion.40
  418.4 3.8 convert_reduce_fusion.1
  434.7 4.7 fusion.71
  442.5 6.0 convolution_convert_fusion.2
  449.4 14.8 %reduce-scatter.23.cloned.1.call-done = f32[96,768]{1,0:T(8,128)} async-done(((f32[768,768]{1,0:T(8,128)}), f32[96,768]{1,0:T(8,128)}) %reduce-scatter.23.cloned.1.call-update) | async-done | bytes 294928 | tf_op jit(solution)/shard_map/reduce_scatter | solution.py:252
  465.8 70.2 %reduce-scatter.25.cloned.1.call-done = f32[96,768]{1,0:T(8,128)} async-done(((f32[768,768]{1,0:T(8,128)}), f32[96,768]{1,0:T(8,128)}) %reduce-scatter.25.cloned.1.call-update) | async-done | bytes 294928 | tf_op jit(solution)/shard_map/reduce_scatter | solution.py:253
  538.2 63.0 %reduce-scatter.21.cloned.1.call-done = f32[96,192]{1,0:T(8,128)} async-done(((f32[768,192]{1,0:T(8,128)}), f32[96,192]{1,0:T(8,128)}) %reduce-scatter.21.cloned.1.call-update) | async-done | bytes 73744 | tf_op jit(solution)/shard_map/reduce_scatter | solution.py:251
  602.8 69.8 %reduce-scatter.19.cloned.1.call-done = f32[96,3,192]{2,0,1:T(8,128)} async-done(((f32[768,3,192]{2,0,1:T(8,128)}), f32[96,3,192]{2,0,1:T(8,128)}) %reduce-scatter.19.cloned.1.call-update) | async-done | bytes 221200 | tf_op jit(solution)/shard_map/reduce_scatter | solution.py:250
  676.8 35.3 %reduce-scatter.17.cloned.1.call-done = bf16[512,768]{1,0:T(8,128)(2,1)} async-done(((bf16[2048,768]{1,0:T(8,128)(2,1)}), bf16[512,768]{1,0:T(8,128)(2,1)}) %reduce-scatter.17.cloned.1.call-update) | async-done | bytes 786448 | tf_op jit(solution)/shard_map/reduce_scatter | solution.py:224
  714.1 39.9 %all-reduce.2 = (f32[4,768]{1,0:T(4,128)S(1)}, f32[8,768]{1,0:T(8,128)S(1)}) all-reduce(f32[4,768]{1,0:T(4,128)S(1)} %pad_maximum_fusion, f32[8,768]{1,0:T(8,128)S(1)} %concatenate.7), channel_id=10, replica_groups=mesh['dp'=8,'mp'=4] {'dp','mp'}, use_global_device_ids=true, to_apply=%region_27.28.clone | all-reduce | flops 9216 | bytes 73728
  756.7 41.3 %psum.7 = f32[]{:T(128)} all-reduce(f32[]{:T(128)S(6)} %add.291), channel_id=1, replica_groups=mesh['dp'=8,'mp'=4] {'dp','mp'}, use_global_device_ids=true, to_apply=%region_36.37 | all-reduce | flops 1 | bytes 8 | tf_op jit(solution)/shard_map/psum | solution.py:259
  (249 shorter events, 94.6 us)
Async XLA Ops:
  8.1 78.1 %all-gather.7.cloned.1.call-start = ((), (), s32[]{:S(2)}) async-start(), calls=%async_computation.8 | async-start | bytes 3932160 | tf_op jit(solution)/shard_map/all_gather | solution.py:124
  13.0 139.1 %reduce-scatter.11.cloned.1.call-start = ((), (), s32[]{:S(2)}) async-start(), calls=%async_computation.9 | async-start | bytes 3932160 | tf_op jit(solution)/shard_map/reduce_scatter | solution.py:142
  52.1 33.9 %copy-start.61 = (s32[32]{0:T(128)S(1)}, s32[32]{0:T(128)}, u32[]{:S(2)}) copy-start(s32[32]{0:T(128)} %param.23) | copy-start | bytes 388
  86.2 16.9 %copy-start.55 = (pred[32,64]{1,0:T(8,128)(4,1)}, pred[32,64]{1,0:T(8,128)(4,1)S(1)}, u32[]{:S(2)}) copy-start(pred[32,64]{1,0:T(8,128)(4,1)S(1)} %iota_compare_fusion) | copy-start | bytes 6148
  103.1 4.7 copy-start.7
  114.6 44.4 %all-gather.11.cloned.1.call-start = ((), (), s32[]{:S(2)}) async-start(), calls=%async_computation.11 | async-start | bytes 1327104 | tf_op jit(solution)/shard_map/all_gather | solution.py:106
  116.2 71.8 %all-gather.9.cloned.1.call-start = ((), (), s32[]{:S(2)}) async-start(), calls=%async_computation.10 | async-start | bytes 3932160 | tf_op jit(solution)/shard_map/all_gather | solution.py:150
  155.6 76.8 %all-gather.13.cloned.1.call-start = ((), (), s32[]{:S(2)}) async-start(), calls=%async_computation.12 | async-start | bytes 1327104 | tf_op jit(solution)/shard_map/all_gather | solution.py:107
  156.3 105.2 %all-gather.15.cloned.1.call-start = ((), (), s32[]{:S(2)}) async-start(), calls=%async_computation.14 | async-start | bytes 3932160 | tf_op jit(solution)/shard_map/all_gather | solution.py:162
  158.3 158.0 %reduce-scatter.15.cloned.1.call-start = ((), (), s32[]{:S(2)}) async-start(), calls=%async_computation.15 | async-start | bytes 3932160 | tf_op jit(solution)/shard_map/reduce_scatter | solution.py:168
  261.5 12.6 %copy-start.62 = (bf16[768,768]{1,0:T(8,128)(2,1)S(1)}, bf16[768,768]{1,0:T(8,128)(2,1)}, u32[]{:S(2)}) copy-start(bf16[768,768]{1,0:T(8,128)(2,1)} %all-gather.11.cloned.1.call-done) | copy-start | bytes 3538948
  278.1 78.5 %reduce-scatter.13.cloned.1.call-start = ((), (), s32[]{:S(2)}) async-start(), calls=%async_computation.13 | async-start | bytes 3932160 | tf_op jit(solution)/shard_map/reduce_scatter | solution.py:157
  284.7 106.3 %all-gather.17.cloned.1.call-start = ((), (), s32[]{:S(2)}) async-start(), calls=%async_computation.16 | async-start | bytes 3932160 | tf_op jit(solution)/shard_map/all_gather | solution.py:178
  316.2 40.4 %copy-start.10 = (bf16[512,768]{1,0:T(8,128)(2,1)S(1)}, bf16[512,768]{1,0:T(8,128)(2,1)}, u32[]{:S(2)}) copy-start(bf16[512,768]{1,0:T(8,128)(2,1)} %reduce-scatter.15.cloned.1.call-done) | copy-start | bytes 2359300
  362.5 101.7 %reduce-scatter.23.cloned.1.call-start = ((), (), s32[]{:S(2)}) async-start(), calls=%async_computation.20 | async-start | bytes 2654208 | tf_op jit(solution)/shard_map/reduce_scatter | solution.py:252
  369.6 166.5 %reduce-scatter.25.cloned.1.call-start = ((), (), s32[]{:S(2)}) async-start(), calls=%async_computation.21 | async-start | bytes 2654208 | tf_op jit(solution)/shard_map/reduce_scatter | solution.py:253
  377.2 224.1 %reduce-scatter.21.cloned.1.call-start = ((), (), s32[]{:S(2)}) async-start(), calls=%async_computation.19 | async-start | bytes 884736 | tf_op jit(solution)/shard_map/reduce_scatter | solution.py:251
  422.3 250.3 %reduce-scatter.19.cloned.1.call-start = ((), (), s32[]{:S(2)}) async-start(), calls=%async_computation.18 | async-start | bytes 2654208 | tf_op jit(solution)/shard_map/reduce_scatter | solution.py:250
  441.4 270.7 %reduce-scatter.17.cloned.1.call-start = ((), (), s32[]{:S(2)}) async-start(), calls=%async_computation.17 | async-start | bytes 3932160 | tf_op jit(solution)/shard_map/reduce_scatter | solution.py:224
  448.5 89.2 %copy-start.52 = (f32[768]{0:T(1024)S(1)}, f32[768]{0:T(1024)}, u32[]{:S(2)}) copy-start(f32[768]{0:T(1024)} %get-tuple-element.31) | copy-start | bytes 9220
  448.5 89.2 %copy-start.51 = (f32[768]{0:T(1024)S(1)}, f32[768]{0:T(1024)}, u32[]{:S(2)}) copy-start(f32[768]{0:T(1024)} %get-tuple-element.38) | copy-start | bytes 9220
  448.5 89.2 %copy-start.54 = (f32[768]{0:T(1024)S(1)}, f32[768]{0:T(1024)}, u32[]{:S(2)}) copy-start(f32[768]{0:T(1024)} %get-tuple-element.75) | copy-start | bytes 9220
  448.5 89.2 %copy-start.53 = (f32[768]{0:T(1024)S(1)}, f32[768]{0:T(1024)}, u32[]{:S(2)}) copy-start(f32[768]{0:T(1024)} %get-tuple-element.83) | copy-start | bytes 9220
  448.5 263.5 %copy-start.42 = (f32[512]{0:T(512)S(1)}, f32[512]{0:T(512)}, u32[]{:S(2)}) copy-start(f32[512]{0:T(512)} %copy-done.41) | copy-start | bytes 6148
  448.5 263.5 %copy-start.47 = (f32[512]{0:T(512)S(1)}, f32[512]{0:T(512)}, u32[]{:S(2)}) copy-start(f32[512]{0:T(512)} %copy-done.46) | copy-start | bytes 6148
  448.6 350.2 %copy-start.44 = (f32[8,768]{1,0:T(8,128)S(1)}, f32[8,768]{1,0:T(8,128)}, u32[]{:S(2)}) copy-start(f32[8,768]{1,0:T(8,128)} %param.39) | copy-start | bytes 73732
  448.6 350.2 %copy-start.56 = (f32[8,24]{1,0:T(8,128)S(1)}, f32[8,24]{1,0:T(8,128)}, u32[]{:S(2)}) copy-start(f32[8,24]{1,0:T(8,128)} %param.40) | copy-start | bytes 2308
  448.6 350.2 %copy-start.57 = (f32[8,24]{1,0:T(8,128)S(1)}, f32[8,24]{1,0:T(8,128)}, u32[]{:S(2)}) copy-start(f32[8,24]{1,0:T(8,128)} %param.41) | copy-start | bytes 2308
  448.6 350.9 %copy-start.59 = (f32[4,24]{1,0:T(4,128)S(1)}, f32[4,24]{1,0:T(4,128)}, u32[]{:S(2)}) copy-start(f32[4,24]{1,0:T(4,128)} %param.37) | copy-start | bytes 1156
  448.6 350.9 %copy-start.60 = (f32[4,24]{1,0:T(4,128)S(1)}, f32[4,24]{1,0:T(4,128)}, u32[]{:S(2)}) copy-start(f32[4,24]{1,0:T(4,128)} %param.38) | copy-start | bytes 1156
  448.6 352.2 %copy-start.5 = (f32[512,768]{1,0:T(8,128)S(1)}, f32[512,768]{1,0:T(8,128)}, u32[]{:S(2)}) copy-start(f32[512,768]{1,0:T(8,128)} %copy-done.4) | copy-start | bytes 4718596
  712.1 88.8 %copy-start.12 = (bf16[512,768]{1,0:T(8,128)(2,1)S(1)}, bf16[512,768]{1,0:T(8,128)(2,1)}, u32[]{:S(2)}) copy-start(bf16[512,768]{1,0:T(8,128)(2,1)} %reduce-scatter.17.cloned.1.call-done) | copy-start | bytes 2359300
  (47 other events, 97.9 us)
Sparse Core Ops, SparseCore 0:
  13.1 31.2 all-gather.6
  114.7 37.3 reduce-scatter.10
  278.3 37.9 reduce-scatter.14
  318.6 37.9 reduce-scatter.12
Sparse Core Ops, SparseCore 1:
  118.1 40.9 all-gather.10
  161.1 26.8 all-gather.8
  190.9 41.5 all-gather.12
  234.6 26.8 all-gather.14
  362.6 28.3 all-gather.16
  394.9 69.2 reduce-scatter.22
  467.9 68.0 reduce-scatter.24
  539.5 61.6 reduce-scatter.20
  604.6 67.9 reduce-scatter.18
  675.1 36.9 reduce-scatter.16
where the time goes:
time: 827 us; the launch traced here: 816 us
  waiting for transfers between devices  465 us (56%)
  blocking collectives  151 us (18%)
  matrix products  84.2 us (10%)
  local copies, waits for them, and re-layouts  51.5 us (6%)
  other arithmetic  40.1 us (5%)
  between operations  22.5 us (3%)
    reduce_scatter x1, waiting for transfers between devices, body(): lax.psum_scatter(down_grad, 'dp', scatter_dimension=0, tiled=True)  70.2 us
    reduce_scatter x1, waiting for transfers between devices, body(): lax.psum_scatter(input_weight_grad, 'dp', scatter_dimension=0, tiled=True)  69.8 us
    reduce_scatter x1, waiting for transfers between devices, body(): lax.psum_scatter(output_grad, 'dp', scatter_dimension=0, tiled=True)  63 us
    psum x1, blocking collectives, body(): grad_norm = jnp.sqrt(lax.psum(local_squares, ('dp', 'mp')))  41.3 us
    unnamed x1, blocking collectives  39.9 us
    all_gather x1, blocking collectives, body(): lax.all_gather(attn_input.astype(jnp.bfloat16), 'dp', axis=0, tiled=True)  38.9 us
    all_gather x1, waiting for transfers between devices, body(): lax.all_gather(mlp_down.astype(jnp.bfloat16), 'dp', axis=0, tiled=True)  36.9 us
    reduce_scatter x1, waiting for transfers between devices, body(): lax.psum_scatter(contract_cols(hidden, full_down).astype(jnp.bfloat16), '...  36.5 us
  transfers between devices with their start and end apart: 14, of which 13 were waited for; matrix products, arithmetic and copies ran while one was open for 13% of the time, Pallas kernels for 0%

commit v1 on v0

v1 whole, which is shorter than its diff:
```python
import functools
import math

import jax
import jax.numpy as jnp
import numpy as np
from jax import lax
from jax.experimental import pallas as pl
from jax.experimental.pallas import tpu as pltpu
from jax.sharding import Mesh, PartitionSpec as P

HEAD = 64
STEP = 10

norm_eps = 1e-06
beta_first = 0.5
beta_second = 0.5
adam_eps = 1e-08
matrix_rate = 0.03
small_rate = 0.3
matrix_decay = 0.01
clip_limit = 1.0
masked_score = -1e30

f32 = jnp.float32
bf16 = jnp.bfloat16
AXES = ("z", "x", "y", "c")
VMEM_LIMIT = 56 * 1024 * 1024
PAIR = 2 * HEAD
GELU_A = math.sqrt(2.0 / math.pi)
GELU_B = 0.044715


class Plan:
    def __init__(self, dims):
        self.dims = dims
        self.z = dims[0]
        self.zbits = [1 << i for i in range(int(math.log2(self.z)))]
        places = [tuple(p) for p in np.ndindex(*dims)]

        def perm(move):
            index = {p: i for i, p in enumerate(places)}
            return [(index[p], index[move(*p)]) for p in places]

        self.to_core = perm(lambda z, x, y, c: (z, x, y, 1 - c))
        self.to_a = perm(lambda z, x, y, c: (z, x ^ (1 - c), y ^ c, c))
        self.to_b = perm(lambda z, x, y, c: (z, x ^ c, y ^ (1 - c), c))
        self.to_z = [
            perm(lambda z, x, y, c, bit=bit: (z ^ bit, x, y, c)) for bit in self.zbits
        ]
        self.slots = [
            (pc, br, ar, zr)
            for pc in range(2)
            for br in range(2)
            for ar in range(2)
            for zr in range(self.z)
        ]

    def send(self, value, perm):
        return lax.ppermute(value, AXES, perm)

    def table(self):
        me = [lax.axis_index(axis) for axis in AXES]
        pc, br, ar, zr = (jnp.asarray(v, jnp.int32) for v in zip(*self.slots))
        core = me[3] ^ pc
        x = me[1] ^ jnp.where(core == 0, ar, br)
        y = me[2] ^ jnp.where(core == 0, br, ar)
        dp = (me[0] ^ zr) * self.dims[1] + x
        mp = y * 2 + core
        return mp * (self.z * self.dims[1]) + dp

    def gather(self, shard):
        block = shard[None]
        for to_z in self.to_z:
            block = jnp.concatenate([block, self.send(block, to_z)], axis=0)
        from_a = self.send(block, self.to_a)
        from_b = self.send(block, self.to_b)
        from_ab = self.send(from_a, self.to_b)
        own = [block, from_a, from_b, from_ab]
        return own + [self.send(piece, self.to_core) for piece in own]

    def reduce(self, own, other, wire):
        z = self.z

        def up(v):
            return v.astype(f32)

        from_core = self.send(other, self.to_core)
        part = up(own[2 * z :]) + up(from_core[2 * z :])
        from_b = self.send(part.astype(wire), self.to_b)
        part = up(own[z : 2 * z]) + up(from_core[z : 2 * z]) + up(from_b[z:])
        from_a = self.send(part.astype(wire), self.to_a)
        total = up(own[:z]) + up(from_core[:z]) + up(from_b[:z]) + up(from_a)
        for bit, to_z in zip(reversed(self.zbits), reversed(self.to_z)):
            received = self.send(total[bit:].astype(wire), to_z)
            total = total[:bit] + up(received)
        return total[0]

    def all_sum(self, value):
        for perm in [self.to_core, self.to_a, self.to_b] + self.to_z:
            value = value + self.send(value, perm)
        return value


def dot(left, right):
    return lax.dot_general(left, right, (((1,), (0,)), ((), ())), preferred_element_type=f32)


def dot_cols(left, right):
    return lax.dot_general(left, right, (((1,), (1,)), ((), ())), preferred_element_type=f32)


def dot_rows(left, right):
    return lax.dot_general(left, right, (((0,), (0,)), ((), ())), preferred_element_type=f32)


def low_lanes(shape):
    return lax.broadcasted_iota(jnp.int32, shape, len(shape) - 1) < HEAD


def swap(value):
    return pltpu.roll(value, HEAD, axis=1)


def moments(rows):
    center = jnp.mean(rows, axis=1, keepdims=True)
    centered = rows - center
    spread = jnp.mean(centered * centered, axis=1, keepdims=True)
    inverse = lax.rsqrt(spread + norm_eps)
    return centered * inverse, inverse


def norm_back(grad_rows, normed, inverse, gain):
    scaled = grad_rows * gain
    return inverse * (
        scaled
        - jnp.mean(scaled, axis=1, keepdims=True)
        - normed * jnp.mean(scaled * normed, axis=1, keepdims=True)
    )


def start_loads(table, pieces, weight, sems, rows, blocks_dp):
    slot = 0
    for piece in pieces:
        for i in range(piece.shape[0]):
            block = table[slot]
            mp = lax.div(block, blocks_dp)
            row = pl.multiple_of(lax.rem(block, blocks_dp) * rows, 16)
            pltpu.make_async_copy(
                piece.at[i], weight.at[mp, pl.ds(row, rows), :], sems.at[mp]
            ).start()
            slot += 1


def wait_load(weight, sems, mp):
    pltpu.make_async_copy(weight.at[mp], weight.at[mp], sems.at[mp]).wait()


def store_blocks(place, stage, step, own, other, sem, rows, dims):
    mz, mx, my, mc = (place[i] for i in range(4))
    pc, yr = 1 - step // 2, step % 2
    target = other if pc else own
    core = mc ^ pc
    z = dims[0]
    for xr in range(2):
        ar = jnp.where(core == 0, xr, yr)
        br = jnp.where(core == 0, yr, xr)
        for zr in range(z):
            dp = (mz ^ zr) * dims[1] + (mx ^ xr)
            row = pl.multiple_of(dp * rows, 16)
            pltpu.make_async_copy(
                stage.at[pl.ds(row, rows), :], target.at[br * (2 * z) + ar * z + zr], sem
            ).start()


def step_mp(place, step):
    pc, yr = 1 - step // 2, step % 2
    return (place[2] ^ yr) * 2 + (place[3] ^ pc)


class Matrix:
    def __init__(self, plan, width, rows):
        self.plan = plan
        self.width = width
        self.rows = rows
        self.direct = rows % 16 == 0
        self.blocks_dp = plan.dims[0] * plan.dims[1]

    def weight_arg(self, pieces, table):
        if self.direct:
            return pieces, table
        stacked = jnp.concatenate(pieces, axis=0)
        order = jnp.argsort(table)
        whole = jnp.take(stacked, order, axis=0)
        whole = whole.reshape(4, self.width, whole.shape[-1])
        return [whole], jnp.arange(4, dtype=jnp.int32)

    def load(self, table, pieces, weight, sems):
        if self.direct:
            start_loads(table, pieces, weight, sems, self.rows, self.blocks_dp)
        else:
            start_loads(table, pieces, weight, sems, self.width, 1)

    def grad_shapes(self, cols):
        if self.direct:
            count = 4 * self.plan.z
            return [jax.ShapeDtypeStruct((count, self.rows, cols), bf16)] * 2
        return [jax.ShapeDtypeStruct((4, self.width, cols), bf16)]

    def store(self, place, stage, step, outs, sem):
        if self.direct:
            store_blocks(place, stage, step, outs[0], outs[1], sem, self.rows, self.plan.dims)
        else:
            pltpu.make_async_copy(stage, outs[0].at[step_mp(place, step)], sem).start()

    def grad_result(self, outs, table):
        if self.direct:
            return outs[0], outs[1]
        whole = outs[0].reshape(4 * self.blocks_dp, self.rows, outs[0].shape[-1])
        half = table.shape[0] // 2
        return jnp.take(whole, table[:half], axis=0), jnp.take(whole, table[half:], axis=0)


def any_spec():
    return pl.BlockSpec(memory_space=pl.ANY)


def vmem_spec():
    return pl.BlockSpec(memory_space=pltpu.VMEM)


def smem_spec():
    return pl.BlockSpec(memory_space=pltpu.SMEM)


def call(kernel, name, args, specs, outs, out_specs, scratch, flops):
    moved = sum(math.prod(a.shape) * a.dtype.itemsize for a in list(args) + list(outs))
    return pl.pallas_call(
        kernel,
        name=name,
        out_shape=outs,
        in_specs=specs,
        out_specs=out_specs,
        scratch_shapes=scratch,
        compiler_params=pltpu.CompilerParams(vmem_limit_bytes=VMEM_LIMIT),
        cost_estimate=pl.CostEstimate(flops=int(flops), bytes_accessed=int(moved), transcendentals=0),
    )(*args)


def attention_forward(matrix, count, width, pieces_n):
    row_block = 256 if count % 256 == 0 else count

    def kernel(*refs):
        table, lens, x_ref, norm_ref, qb_ref, vb_ref, ob_ref = refs[:7]
        pieces = refs[7 : 7 + pieces_n]
        n1_ref, q_ref, k_ref, v_ref, p_ref, a_ref, mid_ref, n2_ref = refs[7 + pieces_n : 15 + pieces_n]
        weight, tail, att, sems = refs[15 + pieces_n :]
        matrix.load(table, pieces, weight, sems)
        gain1, shift1 = norm_ref[0:1, :], norm_ref[1:2, :]
        for r in range(0, count, row_block):
            normed, _ = moments(x_ref[r : r + row_block, :].astype(f32))
            n1_ref[r : r + row_block, :] = (normed * gain1 + shift1).astype(bf16)
        for mp in range(4):
            wait_load(weight, sems, mp)

            def rows_of(i, _, mp=mp):
                at = pl.ds(pl.multiple_of(i * row_block, row_block), row_block)
                joined = dot(n1_ref[at, :], weight[mp, :, 0 : 5 * PAIR])
                q_ref[mp, at, :] = (joined[:, 0:PAIR] + qb_ref[mp : mp + 1, :]).astype(bf16)
                k_ref[mp, at, :] = joined[:, PAIR : 2 * PAIR].astype(bf16)
                v_ref[mp, at, :] = (joined[:, 2 * PAIR : 3 * PAIR] + vb_ref[mp : mp + 1, :]).astype(bf16)
                if mp % 2 == 0:
                    tail[at, :] = joined[:, 3 * PAIR :]
                else:
                    pair = 4 + mp // 2
                    low = low_lanes((row_block, PAIR))
                    even3, even4 = tail[at, 0:PAIR], tail[at, PAIR:]
                    odd3, odd4 = joined[:, 3 * PAIR : 4 * PAIR], joined[:, 4 * PAIR :]
                    query = jnp.where(low, even3, swap(odd3)) + qb_ref[pair : pair + 1, :]
                    value = jnp.where(low, even4, swap(odd4)) + vb_ref[pair : pair + 1, :]
                    q_ref[pair, at, :] = query.astype(bf16)
                    k_ref[pair, at, :] = jnp.where(low, swap(even3), odd3).astype(bf16)
                    v_ref[pair, at, :] = value.astype(bf16)
                return 0

            lax.fori_loop(0, count // row_block, rows_of, 0)

        blocks = count // PAIR
        lane = lax.broadcasted_iota(jnp.int32, (2 * PAIR, PAIR), 1)
        line = lax.broadcasted_iota(jnp.int32, (2 * PAIR, PAIR), 0)
        same = ((line // HEAD) % 2) == (lane // HEAD)
        low = low_lanes((PAIR, PAIR))
        zero = jnp.zeros((PAIR, PAIR), bf16)

        def attend(i, _):
            r = lax.div(i, 6)
            pair = lax.rem(i, 6)
            at = pl.ds(pl.multiple_of(r * PAIR, PAIR), PAIR)
            query = q_ref[pair, at, :]
            stacked = jnp.concatenate([jnp.where(low, query, zero), jnp.where(low, zero, query)], axis=0)
            scores = dot_cols(stacked, k_ref[pair, at, :]) * (HEAD ** (-0.5))
            limit = jnp.where(lane < HEAD, lens[2 * r], lens[2 * r + 1] + HEAD)
            scores = jnp.where(same & (lane < limit), scores, masked_score)
            expo = jnp.exp(scores - jnp.max(scores, axis=1, keepdims=True))
            probs = (expo / jnp.sum(expo, axis=1, keepdims=True)).astype(bf16)
            p_ref[i] = probs
            out = dot(probs, v_ref[pair, at, :])
            att[pair, at, :] = jnp.where(low, out[0:PAIR], out[PAIR:])
            return 0

        lax.fori_loop(0, 6 * blocks, attend, 0, unroll=2)
        low_all = low_lanes((count, PAIR))
        for mp in range(4):
            second = att[4 + mp // 2]
            second = swap(second) if mp % 2 == 0 else second
            a_ref[mp, :, 0:PAIR] = jnp.where(low_all, 0.0, second).astype(bf16)
            a_ref[mp, :, PAIR:] = att[mp].astype(bf16)

        gain2, shift2 = norm_ref[2:3, :], norm_ref[3:4, :]

        def finish(i, _):
            at = pl.ds(pl.multiple_of(i * row_block, row_block), row_block)
            branch = x_ref[at, :].astype(f32) + ob_ref[...]
            for mp in range(4):
                branch = branch + dot_cols(a_ref[mp, at, :], weight[mp, :, 4 * PAIR :])
            mid_ref[at, :] = branch
            normed, _ = moments(branch)
            n2_ref[at, :] = (normed * gain2 + shift2).astype(bf16)
            return 0

        lax.fori_loop(0, count // row_block, finish, 0)

    outs = [
        jax.ShapeDtypeStruct((count, width), bf16),
        jax.ShapeDtypeStruct((6, count, PAIR), bf16),
        jax.ShapeDtypeStruct((6, count, PAIR), bf16),
        jax.ShapeDtypeStruct((6, count, PAIR), bf16),
        jax.ShapeDtypeStruct((6 * (count // PAIR), 2 * PAIR, PAIR), bf16),
        jax.ShapeDtypeStruct((4, count, 2 * PAIR), bf16),
        jax.ShapeDtypeStruct((count, width), f32),
        jax.ShapeDtypeStruct((count, width), bf16),
    ]
    scratch = [
        pltpu.VMEM((4, width, 6 * PAIR), bf16),
        pltpu.VMEM((count, 2 * PAIR), f32),
        pltpu.VMEM((6, count, PAIR), f32),
        pltpu.SemaphoreType.DMA((4,)),
    ]
    return kernel, outs, scratch


def mlp_forward(matrix, count, width, pieces_n):
    row_block = 256 if count % 256 == 0 else count

    def kernel(*refs):
        table, place, n2_ref, glow_ref, ub_ref = refs[:5]
        pieces = refs[5 : 5 + pieces_n]
        h_ref, gp_ref = refs[5 + pieces_n : 7 + pieces_n]
        n_grads = 2 if matrix.direct else 1
        grads = refs[7 + pieces_n : 7 + pieces_n + n_grads]
        weight, stage, sems, out_sem = refs[7 + pieces_n + n_grads :]
        matrix.load(table, pieces, weight, sems)
        for step in range(4):
            mp = step_mp(place, step)
            wait_load(weight, sems, mp)

            def rows_of(i, _):
                at = pl.ds(pl.multiple_of(i * row_block, row_block), row_block)
                value = dot(n2_ref[at, :], weight[mp]) + ub_ref[mp]
                square = value * value
                inner = (GELU_A * value) * (1.0 + GELU_B * square)
                t = jnp.tanh(inner)
                half = 0.5 * (1.0 + t)
                h_ref[mp, at, :] = (value * half).astype(bf16)
                slope = half + (0.5 * GELU_A) * value * (1.0 - t * t) * (1.0 + (3.0 * GELU_B) * square)
                gp_ref[mp, at, :] = slope.astype(bf16)
                return 0

            lax.fori_loop(0, count // row_block, rows_of, 0)
            stage[step] = dot_rows(glow_ref[...], h_ref[mp]).astype(bf16)
            matrix.store(place, stage.at[step], step, grads, out_sem)
        pltpu.make_async_copy(stage, stage, out_sem).wait()

    outs = [
        jax.ShapeDtypeStruct((4, count, width), bf16),
        jax.ShapeDtypeStruct((4, count, width), bf16),
    ] + matrix.grad_shapes(width)
    scratch = [
        pltpu.VMEM((4, width, width), bf16),
        pltpu.VMEM((4, width, width), bf16),
        pltpu.SemaphoreType.DMA((4,)),
        pltpu.SemaphoreType.DMA,
    ]
    return kernel, outs, scratch


def mlp_backward(matrix, count, width, pieces_n):
    row_block = 256 if count % 256 == 0 else count

    def kernel(*refs):
        table, place, glow_ref, gp_ref, n2_ref = refs[:5]
        pieces = refs[5 : 5 + pieces_n]
        eg_ref, ubg_ref = refs[5 + pieces_n : 7 + pieces_n]
        n_grads = 2 if matrix.direct else 1
        grads = refs[7 + pieces_n : 7 + pieces_n + n_grads]
        weight, stage, sems, out_sem = refs[7 + pieces_n + n_grads :]
        matrix.load(table, pieces, weight, sems)
        for step in range(4):
            mp = step_mp(place, step)
            wait_load(weight, sems, mp)

            def rows_of(i, total):
                at = pl.ds(pl.multiple_of(i * row_block, row_block), row_block)
                grad = dot(glow_ref[at, :], weight[mp]) * gp_ref[mp, at, :].astype(f32)
                grad = grad.astype(bf16)
                eg_ref[mp, at, :] = grad
                return total + jnp.sum(grad.astype(f32), axis=0, keepdims=True)

            ubg_ref[mp] = lax.fori_loop(
                0, count // row_block, rows_of, jnp.zeros((1, width), f32)
            )
            stage[step] = dot_rows(n2_ref[...], eg_ref[mp]).astype(bf16)
            matrix.store(place, stage.at[step], step, grads, out_sem)
        pltpu.make_async_copy(stage, stage, out_sem).wait()

    outs = [
        jax.ShapeDtypeStruct((4, count, width), bf16),
        jax.ShapeDtypeStruct((4, 1, width), f32),
    ] + matrix.grad_shapes(width)
    scratch = [
        pltpu.VMEM((4, width, width), bf16),
        pltpu.VMEM((4, width, width), bf16),
        pltpu.SemaphoreType.DMA((4,)),
        pltpu.SemaphoreType.DMA,
    ]
    return kernel, outs, scratch


def middle_backward(matrix, count, width, pieces_n):
    row_block = 256 if count % 256 == 0 else count

    def kernel(*refs):
        table, eg_ref, mid_ref, glow_ref, norm_ref = refs[:5]
        pieces = refs[5 : 5 + pieces_n]
        mg_ref, ml_ref, sums_ref, weight, sems = refs[5 + pieces_n :]
        matrix.load(table, pieces, weight, sems)
        for mp in range(4):
            wait_load(weight, sems, mp)

        def rows_of(i, total):
            at = pl.ds(pl.multiple_of(i * row_block, row_block), row_block)
            two = dot_cols(eg_ref[0, at, :], weight[0])
            for mp in range(1, 4):
                two = two + dot_cols(eg_ref[mp, at, :], weight[mp])
            normed, inverse = moments(mid_ref[at, :])
            out_grad = glow_ref[at, :].astype(f32)
            grad = out_grad + norm_back(two, normed, inverse, norm_ref[2:3, :])
            mg_ref[at, :] = grad
            ml_ref[at, :] = grad.astype(bf16)
            lines = [two * normed, two, grad, out_grad]
            lines = [jnp.sum(line, axis=0, keepdims=True) for line in lines]
            return total + jnp.concatenate(lines, axis=0)

        sums_ref[...] = lax.fori_loop(0, count // row_block, rows_of, jnp.zeros((4, width), f32))

    outs = [
        jax.ShapeDtypeStruct((count, width), f32),
        jax.ShapeDtypeStruct((count, width), bf16),
        jax.ShapeDtypeStruct((4, width), f32),
    ]
    scratch = [pltpu.VMEM((4, width, width), bf16), pltpu.SemaphoreType.DMA((4,))]
    return kernel, outs, scratch


def block_out(matrix, count, width, pieces_n):
    row_block = 256 if count % 256 == 0 else count

    def kernel(*refs):
        table, h_ref, mid_ref, bias_ref = refs[:4]
        pieces = refs[4 : 4 + pieces_n]
        out_ref, weight, sems = refs[4 + pieces_n :]
        matrix.load(table, pieces, weight, sems)
        for mp in range(4):
            wait_load(weight, sems, mp)

        def rows_of(i, _):
            at = pl.ds(pl.multiple_of(i * row_block, row_block), row_block)
            total = mid_ref[at, :] + bias_ref[...]
            for mp in range(4):
                total = total + dot_cols(h_ref[mp, at, :], weight[mp])
            out_ref[at, :] = total.astype(bf16)
            return 0

        lax.fori_loop(0, count // row_block, rows_of, 0)

    outs = [jax.ShapeDtypeStruct((count, width), bf16)]
    scratch = [pltpu.VMEM((4, width, width), bf16), pltpu.SemaphoreType.DMA((4,))]
    return kernel, outs, scratch


def attention_backward(matrix, count, width, pieces_n):
    row_block = 256 if count % 256 == 0 else count

    def kernel(*refs):
        table, place, ml_ref, a_ref, q_ref, k_ref, v_ref, p_ref, n1_ref = refs[:9]
        pieces = refs[9 : 9 + pieces_n]
        dj_ref, qs_ref, vs_ref = refs[9 + pieces_n : 12 + pieces_n]
        n_grads = 2 if matrix.direct else 1
        grads = refs[12 + pieces_n : 12 + pieces_n + n_grads]
        weight, tail, da, dq, dk, dv, stage, sems, out_sem = refs[12 + pieces_n + n_grads :]
        matrix.load(table, pieces, weight, sems)
        for mp in range(4):
            wait_load(weight, sems, mp)

            def rows_of(i, _, mp=mp):
                at = pl.ds(pl.multiple_of(i * row_block, row_block), row_block)
                grad = dot(ml_ref[at, :], weight[mp, :, 4 * PAIR :])
                da[mp, at, :] = grad[:, PAIR:].astype(bf16)
                if mp % 2 == 0:
                    tail[at, :] = grad[:, 0:PAIR]
                else:
                    low = low_lanes((row_block, PAIR))
                    both = jnp.where(low, swap(tail[at, :]), grad[:, 0:PAIR])
                    da[4 + mp // 2, at, :] = both.astype(bf16)
                return 0

            lax.fori_loop(0, count // row_block, rows_of, 0)

        low = low_lanes((PAIR, PAIR))
        zero = jnp.zeros((PAIR, PAIR), bf16)

        def stack(value):
            return jnp.concatenate([jnp.where(low, value, zero), jnp.where(low, zero, value)], axis=0)

        def attend(i, _):
            r = lax.div(i, 6)
            pair = lax.rem(i, 6)
            at = pl.ds(pl.multiple_of(r * PAIR, PAIR), PAIR)
            grad = stack(da[pair, at, :])
            low_probs = p_ref[i]
            probs = low_probs.astype(f32)
            probs_grad = dot_cols(grad, v_ref[pair, at, :])
            shared = jnp.sum(probs * probs_grad, axis=1, keepdims=True)
            scores_grad = (probs * (probs_grad - shared)).astype(bf16)
            dv[pair, at, :] = dot_rows(low_probs, grad)
            both = dot(scores_grad, k_ref[pair, at, :])
            scale = HEAD ** (-0.5)
            dq[pair, at, :] = jnp.where(low, both[0:PAIR], both[PAIR:]) * scale
            dk[pair, at, :] = dot_rows(scores_grad, stack(q_ref[pair, at, :])) * scale
            return 0

        lax.fori_loop(0, 6 * (count // PAIR), attend, 0, unroll=2)
        for pair in range(6):
            qs_ref[pair : pair + 1, :] = jnp.sum(dq[pair].astype(bf16).astype(f32), axis=0, keepdims=True)
            vs_ref[pair : pair + 1, :] = jnp.sum(dv[pair].astype(bf16).astype(f32), axis=0, keepdims=True)
        low_all = low_lanes((count, PAIR))
        for mp in range(4):
            dj_ref[mp, :, 0:PAIR] = dq[mp].astype(bf16)
            dj_ref[mp, :, PAIR : 2 * PAIR] = dk[mp].astype(bf16)
            dj_ref[mp, :, 2 * PAIR : 3 * PAIR] = dv[mp].astype(bf16)
            query, keys, value = dq[4 + mp // 2], dk[4 + mp // 2], dv[4 + mp // 2]
            if mp % 2 == 0:
                third = jnp.where(low_all, query, swap(keys))
                fourth = jnp.where(low_all, value, 0.0)
            else:
                third = jnp.where(low_all, swap(query), keys)
                fourth = jnp.where(low_all, swap(value), 0.0)
            dj_ref[mp, :, 3 * PAIR : 4 * PAIR] = third.astype(bf16)
            dj_ref[mp, :, 4 * PAIR : 5 * PAIR] = fourth.astype(bf16)
        for step in range(4):
            mp = step_mp(place, step)
            first = dot_rows(n1_ref[...], dj_ref[mp])
            second = dot_rows(ml_ref[...], a_ref[mp])
            stage[step, :, 0 : 4 * PAIR] = first[:, 0 : 4 * PAIR].astype(bf16)
            stage[step, :, 4 * PAIR : 5 * PAIR] = (first[:, 4 * PAIR :] + second[:, 0:PAIR]).astype(bf16)
            stage[step, :, 5 * PAIR :] = second[:, PAIR:].astype(bf16)
            matrix.store(place, stage.at[step], step, grads, out_sem)
        pltpu.make_async_copy(stage, stage, out_sem).wait()

    outs = [
        jax.ShapeDtypeStruct((4, count, 5 * PAIR), bf16),
        jax.ShapeDtypeStruct((6, PAIR), f32),
        jax.ShapeDtypeStruct((6, PAIR), f32),
    ] + matrix.grad_shapes(6 * PAIR)
    scratch = [
        pltpu.VMEM((4, width, 6 * PAIR), bf16),
        pltpu.VMEM((count, PAIR), f32),
        pltpu.VMEM((6, count, PAIR), bf16),
        pltpu.VMEM((6, count, PAIR), f32),
        pltpu.VMEM((6, count, PAIR), f32),
        pltpu.VMEM((6, count, PAIR), f32),
        pltpu.VMEM((4, width, 6 * PAIR), bf16),
        pltpu.SemaphoreType.DMA((4,)),
        pltpu.SemaphoreType.DMA,
    ]
    return kernel, outs, scratch


def input_backward(matrix, count, width, pieces_n):
    row_block = 256 if count % 256 == 0 else count

    def kernel(*refs):
        table, dj_ref, x_ref, mg_ref, norm_ref = refs[:5]
        pieces = refs[5 : 5 + pieces_n]
        out_ref, sums_ref, weight, sems = refs[5 + pieces_n :]
        matrix.load(table, pieces, weight, sems)
        for mp in range(4):
            wait_load(weight, sems, mp)

        def rows_of(i, total):
            at = pl.ds(pl.multiple_of(i * row_block, row_block), row_block)
            one = dot_cols(dj_ref[0, at, :], weight[0, :, 0 : 5 * PAIR])
            for mp in range(1, 4):
                one = one + dot_cols(dj_ref[mp, at, :], weight[mp, :, 0 : 5 * PAIR])
            normed, inverse = moments(x_ref[at, :].astype(f32))
            out_ref[at, :] = mg_ref[at, :] + norm_back(one, normed, inverse, norm_ref[0:1, :])
            lines = [jnp.sum(one * normed, axis=0, keepdims=True), jnp.sum(one, axis=0, keepdims=True)]
            return total + jnp.concatenate(lines, axis=0)

        sums_ref[...] = lax.fori_loop(0, count // row_block, rows_of, jnp.zeros((2, width), f32))

    outs = [
        jax.ShapeDtypeStruct((count, width), f32),
        jax.ShapeDtypeStruct((2, width), f32),
    ]
    scratch = [pltpu.VMEM((4, width, 6 * PAIR), bf16), pltpu.SemaphoreType.DMA((4,))]
    return kernel, outs, scratch


def adam_step(weight, first, second, grad, rate, decay):
    first_new = beta_first * first + (1.0 - beta_first) * grad
    second_new = beta_second * second + (1.0 - beta_second) * grad * grad
    first_hat = first_new / (1.0 - beta_first**STEP)
    second_hat = second_new / (1.0 - beta_second**STEP)
    weight_new = weight - rate * (first_hat / (jnp.sqrt(second_hat) + adam_eps) + decay * weight)
    return (weight_new, first_new, second_new)


def pack_attention(inputs, output):
    q, k, v = inputs[:, 0], inputs[:, 1], inputs[:, 2]
    return jnp.concatenate(
        [
            q[:, :PAIR],
            k[:, :PAIR],
            v[:, :PAIR],
            q[:, PAIR:],
            k[:, PAIR:],
            v[:, PAIR:],
            output[:, PAIR:],
            output[:, :PAIR],
        ],
        axis=1,
    )


def unpack_attention(packed):
    def cut(start, size):
        return packed[:, start : start + size]

    q = jnp.concatenate([cut(0, PAIR), cut(3 * PAIR, HEAD)], axis=1)
    k = jnp.concatenate([cut(PAIR, PAIR), cut(3 * PAIR + HEAD, HEAD)], axis=1)
    v = jnp.concatenate([cut(2 * PAIR, PAIR), cut(4 * PAIR, HEAD)], axis=1)
    output = jnp.concatenate([cut(5 * PAIR, PAIR), cut(4 * PAIR + HEAD, HEAD)], axis=1)
    return jnp.stack([q, k, v], axis=1), output


def to_pairs(line):
    groups = line.reshape(4, 3 * HEAD)
    return jnp.concatenate([groups[:, :PAIR], groups[:, PAIR:].reshape(2, PAIR)], axis=0)


def from_pairs(pairs):
    groups = jnp.concatenate([pairs[:4], pairs[4:].reshape(4, HEAD)], axis=1)
    return groups.reshape(-1)


def body(
    plan,
    block_input,
    cotangent,
    lengths,
    attn_input,
    attn_input_first,
    attn_input_second,
    attn_output,
    attn_output_first,
    attn_output_second,
    mlp_up,
    mlp_up_first,
    mlp_up_second,
    mlp_down,
    mlp_down_first,
    mlp_down_second,
    norm_params,
    norm_first,
    norm_second,
    bias_params,
    bias_first,
    bias_second,
):
    width = norm_params.shape[1]
    units = bias_params.shape[0] - 4
    count = block_input.shape[0]
    shard_rows = attn_input.shape[0]
    place = jnp.stack([lax.axis_index(axis) for axis in AXES]).astype(jnp.int32)
    rank = place[2] * 2 + place[3]
    group = (place[0] * plan.dims[1] + place[1]) * 4 + rank
    captions = lengths.shape[0] // 4
    length = count // captions
    lens = lax.dynamic_slice_in_dim(lengths, rank * captions, captions, 0)
    valid = lax.broadcasted_iota(jnp.int32, (captions, length), 1) < lens[:, None]
    grad_low = jnp.where(valid.reshape(-1, 1), cotangent, jnp.zeros((), bf16))
    matrix = Matrix(plan, width, shard_rows)
    table = plan.table()

    pieces_attn = plan.gather(pack_attention(attn_input.astype(bf16), attn_output.astype(bf16)))
    pieces_up = plan.gather(mlp_up.astype(bf16))
    pieces_down = plan.gather(mlp_down.astype(bf16))
    pieces_attn, order = matrix.weight_arg(pieces_attn, table)
    pieces_up, _ = matrix.weight_arg(pieces_up, table)
    pieces_down, _ = matrix.weight_arg(pieces_down, table)
    pieces_n = len(pieces_attn)
    any_pieces = [any_spec()] * pieces_n
    grads_n = 2 if matrix.direct else 1
    any_grads = [any_spec()] * grads_n
    macs = 2.0 * count * width * width

    kernel, outs, scratch = attention_forward(matrix, count, width, pieces_n)
    n1, q, k, v, probs, a_out, middle, n2 = call(
        kernel,
        "attention_forward",
        [order, lens, block_input, norm_params, to_pairs(bias_params[units]), to_pairs(bias_params[units + 1]), bias_params[units + 2 : units + 3]]
        + pieces_attn,
        [smem_spec()] * 2 + [vmem_spec()] * 5 + any_pieces,
        outs,
        [vmem_spec()] * 8,
        scratch,
        5 * macs,
    )
    kernel, outs, scratch = mlp_forward(matrix, count, width, pieces_n)
    hidden, slope, *down_parts = call(
        kernel,
        "mlp_forward",
        [order, place, n2, grad_low, bias_params[:units].reshape(4, 1, width)] + pieces_up,
        [smem_spec()] * 2 + [vmem_spec()] * 3 + any_pieces,
        outs,
        [vmem_spec()] * 2 + any_grads,
        scratch,
        8 * macs,
    )
    kernel, outs, scratch = mlp_backward(matrix, count, width, pieces_n)
    expanded_grad, up_bias_grad, *up_parts = call(
        kernel,
        "mlp_backward",
        [order, place, grad_low, slope, n2] + pieces_down,
        [smem_spec()] * 2 + [vmem_spec()] * 3 + any_pieces,
        outs,
        [vmem_spec()] * 2 + any_grads,
        scratch,
        8 * macs,
    )
    kernel, outs, scratch = middle_backward(matrix, count, width, pieces_n)
    middle_grad, middle_low, sums_two = call(
        kernel,
        "middle_backward",
        [order, expanded_grad, middle, grad_low, norm_params] + pieces_up,
        [smem_spec()] + [vmem_spec()] * 4 + any_pieces,
        outs,
        [vmem_spec()] * 3,
        scratch,
        4 * macs,
    )
    kernel, outs, scratch = attention_backward(matrix, count, width, pieces_n)
    joined_grad, query_sums, value_sums, *attn_parts = call(
        kernel,
        "attention_backward",
        [order, place, middle_low, a_out, q, k, v, probs, n1] + pieces_attn,
        [smem_spec()] * 2 + [vmem_spec()] * 7 + any_pieces,
        outs,
        [vmem_spec()] * 3 + any_grads,
        scratch,
        7 * macs,
    )
    kernel, outs, scratch = input_backward(matrix, count, width, pieces_n)
    input_grad, sums_one = call(
        kernel,
        "input_backward",
        [order, joined_grad, block_input, middle_grad, norm_params] + pieces_attn,
        [smem_spec()] + [vmem_spec()] * 4 + any_pieces,
        outs,
        [vmem_spec()] * 2,
        scratch,
        3 * macs,
    )
    kernel, outs, scratch = block_out(matrix, count, width, pieces_n)
    (block_output,) = call(
        kernel,
        "block_out",
        [order, hidden, middle, bias_params[units + 3 : units + 4]] + pieces_down,
        [smem_spec()] + [vmem_spec()] * 3 + any_pieces,
        outs,
        [vmem_spec()],
        scratch,
        4 * macs,
    )

    down_sum = plan.reduce(*matrix.grad_result(down_parts, table), bf16)
    up_sum = plan.reduce(*matrix.grad_result(up_parts, table), bf16)
    attn_sum = plan.reduce(*matrix.grad_result(attn_parts, table), bf16)
    input_sum, output_sum = unpack_attention(attn_sum)

    columns = norm_first.shape[1]
    small = jnp.concatenate(
        [
            sums_one,
            sums_two[:2],
            up_bias_grad.reshape(units, width),
            from_pairs(query_sums)[None],
            from_pairs(value_sums)[None],
            sums_two[2:],
        ],
        axis=0,
    )
    lines = small.shape[0]
    blocks = small.reshape(lines, -1, 4, columns).transpose(2, 1, 0, 3).reshape(-1, lines * columns)
    blocks = jnp.take(blocks, table, axis=0)
    half = blocks.shape[0] // 2
    small_sum = plan.reduce(blocks[:half], blocks[half:], f32).reshape(lines, columns)
    norm_sum, bias_sum = small_sum[:4], small_sum[4:]

    reduced = (attn_sum, up_sum, down_sum, small_sum)
    squares = sum(jnp.sum(grad * grad) for grad in reduced)
    grad_norm = jnp.sqrt(plan.all_sum(squares.reshape(1, 1))[0, 0])
    factor = jnp.minimum(1.0, clip_limit / (grad_norm + 1e-06))
    own_norm = lax.dynamic_slice_in_dim(norm_params, group * columns, columns, 1)
    own_bias = lax.dynamic_slice_in_dim(bias_params, group * columns, columns, 1)
    results = [block_output, input_grad, grad_norm]
    matrices = (
        (attn_input, attn_input_first, attn_input_second, input_sum),
        (attn_output, attn_output_first, attn_output_second, output_sum),
        (mlp_up, mlp_up_first, mlp_up_second, up_sum),
        (mlp_down, mlp_down_first, mlp_down_second, down_sum),
    )
    for weight, first, second, grad in matrices:
        clipped = grad * factor
        new, first_new, second_new = adam_step(
            weight, first, second, clipped, matrix_rate, matrix_decay
        )
        results += [clipped, new, first_new, second_new, new.astype(bf16)]
    smalls = (
        (own_norm, norm_first, norm_second, norm_sum),
        (own_bias, bias_first, bias_second, bias_sum),
    )
    for weight, first, second, grad in smalls:
        clipped = grad * factor
        new, first_new, second_new = adam_step(weight, first, second, clipped, small_rate, 0.0)
        results += [clipped, new, first_new, second_new]
    return tuple(results)


def solution(mesh):
    dp, mp = mesh.shape["dp"], mesh.shape["mp"]
    dims = (dp // 2, 2, mp // 2, 2)
    fine = Mesh(np.asarray(mesh.devices).reshape(dims), AXES)
    plan = Plan(dims)
    d, m = ("z", "x"), ("y", "c")
    every = d + m
    rows = P(every, None)
    cube = P(d, None, m)
    flat = P(d, m)
    small = P(None, every)
    return jax.shard_map(
        functools.partial(body, plan),
        mesh=fine,
        in_specs=(rows, rows, P(d)) + (cube,) * 3 + (flat,) * 9 + (P(), small, small) * 2,
        out_specs=(rows, rows, P()) + (cube,) * 5 + (flat,) * 15 + (small,) * 8,
        check_vma=False,
    )
```

time: 827 us -> 346 us (0.42); the launches traced: 816 us -> 346 us
  waiting for transfers between devices: 465 us -> 143 us
  blocking collectives: 151 us -> 0 us
  Pallas kernels: 0 us -> 103 us
  matrix products: 84.2 us -> 0 us
  starting transfers between devices: 1.61 us -> 51.4 us
  local copies, waits for them, and re-layouts: 51.5 us -> 9.89 us
  between operations: 22.5 us -> 8.67 us
  other arithmetic: 40.1 us -> 30.2 us
    reduce_scatter x8 -> x0, waiting for transfers between devices: 356 us -> none  [the longest x1 70.2 us: body(): lax.psum_scatter(down_grad, 'dp', scatter_dimension=0, tiled=True)]
    ppermute x0 -> x52, waiting for transfers between devices: none -> 143 us  [send(): return lax.ppermute(value, AXES, perm)]
    all_gather x6 -> x0, waiting for transfers between devices: 109 us -> none  [the longest x1 36.9 us: body(): lax.all_gather(mlp_down.astype(jnp.bfloat16), 'dp', axis=0, tiled=True)]
    pallas_call x0 -> x7, Pallas kernels: none -> 103 us  [call(): pl.pallas_call(kernel, name=name, out_shape=outs, in_specs=specs, out_spe...]
    dot_general x18 -> x0, matrix products: 84.2 us -> none  [the longest x4 21.1 us: contract_rows(): lax.dot_general(left, right, (((0,), (0,)), ((), ())), preferred_element_...]
    all_gather x2 -> x0, blocking collectives: 70 us -> none  [the longest x1 38.9 us: body(): lax.all_gather(attn_input.astype(jnp.bfloat16), 'dp', axis=0, tiled=True)]
    ppermute x0 -> x52, starting transfers between devices: none -> 51.4 us  [send(): return lax.ppermute(value, AXES, perm)]
    psum x1 -> x0, blocking collectives: 41.3 us -> none  [body(): grad_norm = jnp.sqrt(lax.psum(local_squares, ('dp', 'mp')))]
  transfers between devices with their start and end apart: 14 -> 52, of which waited for: 13 -> 26; matrix products, arithmetic and copies ran while one was open for 13% -> 8% of each run, Pallas kernels for 0% -> 16%
where the time goes in v1:
time: 346 us
  waiting for transfers between devices  143 us (41%)
  Pallas kernels  103 us (30%)
  starting transfers between devices  51.4 us (15%)
  other arithmetic  30.2 us (9%)
  local copies, waits for them, and re-layouts  9.89 us (3%)
  between operations  8.67 us (3%)
    ppermute x52, waiting for transfers between devices, send(): return lax.ppermute(value, AXES, perm)  143 us
    pallas_call x7, Pallas kernels, call(): pl.pallas_call(kernel, name=name, out_shape=outs, in_specs=specs, out_spe...  103 us
    ppermute x52, starting transfers between devices, send(): return lax.ppermute(value, AXES, perm)  51.4 us
  transfers between devices with their start and end apart: 52, of which 26 were waited for; matrix products, arithmetic and copies ran while one was open for 8% of the time, Pallas kernels for 16%

profile of v1, /device:TPU:0, one launch (start us, length us, event | category | flops | bytes accessed | tf_op | source)
XLA Modules:
  0.0 345.5 jit_solution(5080489614405076653)
XLA Ops:
  2.8 3.1 collective-permute-start
  5.9 3.8 %collective-permute-done = bf16[1,96,768]{2,1,0:T(8,128)(2,1)S(1)} collective-permute-done((bf16[1,96,768]{2,1,0:T(8,128)(2,1)S(1)}, bf16[1,96,768]{2,1,0:T(8,128)(2,1)S(1)}, u32[]{:S(2)}, u32[]{:S(2)}) %collective-permute-start) | collective-permute-done | bytes 147488 | tf_op jit(solution)/shard_map/ppermute | solution.py:60
  9.8 2.8 collective-permute-start.1
  14.3 11.0 %collective-permute-done.1 = bf16[2,96,768]{2,1,0:T(8,128)(2,1)S(1)} collective-permute-done((bf16[2,96,768]{2,1,0:T(8,128)(2,1)S(1)}, bf16[2,96,768]{2,1,0:T(8,128)(2,1)S(1)}, u32[]{:S(2)}, u32[]{:S(2)}) %collective-permute-start.1) | collective-permute-done | bytes 294944 | tf_op jit(solution)/shard_map/ppermute | solution.py:60
  29.1 3.4 collective-permute-start.10
  32.7 3.1 collective-permute-start.19
  35.8 16.9 %collective-permute-done.10 = bf16[2,96,768]{2,1,0:T(8,128)(2,1)S(1)} collective-permute-done((bf16[2,96,768]{2,1,0:T(8,128)(2,1)S(1)}, bf16[2,96,768]{2,1,0:T(8,128)(2,1)S(1)}, u32[]{:S(2)}, u32[]{:S(2)}) %collective-permute-start.10) | collective-permute-done | bytes 294944 | tf_op jit(solution)/shard_map/ppermute | solution.py:60
  53.8 4.1 %collective-permute-done.19 = bf16[2,96,768]{2,1,0:T(8,128)(2,1)S(1)} collective-permute-done((bf16[2,96,768]{2,1,0:T(8,128)(2,1)S(1)}, bf16[2,96,768]{2,1,0:T(8,128)(2,1)S(1)}, u32[]{:S(2)}, u32[]{:S(2)}) %collective-permute-start.19) | collective-permute-done | bytes 294944 | tf_op jit(solution)/shard_map/ppermute | solution.py:60
  60.6 5.5 %collective-permute-done.11.refs_6_ = bf16[4,96,768]{2,1,0:T(8,128)(2,1)} collective-permute-done((bf16[4,96,768]{2,1,0:T(8,128)(2,1)S(1)}, bf16[4,96,768]{2,1,0:T(8,128)(2,1)}, u32[]{:S(2)}, u32[]{:S(2)}) %collective-permute-start.11) | collective-permute-done | bytes 589856 | tf_op jit(solution)/shard_map/ppermute | solution.py:60
  66.0 7.8 %collective-permute-done.12.refs_7_ = bf16[4,96,768]{2,1,0:T(8,128)(2,1)S(1)} collective-permute-done((bf16[4,96,768]{2,1,0:T(8,128)(2,1)S(1)}, bf16[4,96,768]{2,1,0:T(8,128)(2,1)S(1)}, u32[]{:S(2)}, u32[]{:S(2)}) %collective-permute-start.12) | collective-permute-done | bytes 589856 | tf_op jit(solution)/shard_map/ppermute | solution.py:60
  74.4 4.2 %collective-permute-done.20.refs_5_.refs_6_ = bf16[4,96,768]{2,1,0:T(8,128)(2,1)S(1)} collective-permute-done((bf16[4,96,768]{2,1,0:T(8,128)(2,1)S(1)}, bf16[4,96,768]{2,1,0:T(8,128)(2,1)S(1)}, u32[]{:S(2)}, u32[]{:S(2)}) %collective-permute-start.20) | collective-permute-done | bytes 589856 | tf_op jit(solution)/shard_map/ppermute | solution.py:60
  81.9 4.9 %collective-permute-done.4.refs_10_.refs_12_.refs_8_ = bf16[4,96,768]{2,1,0:T(8,128)(2,1)} collective-permute-done((bf16[4,96,768]{2,1,0:T(8,128)(2,1)}, bf16[4,96,768]{2,1,0:T(8,128)(2,1)}, u32[]{:S(2)}, u32[]{:S(2)}) %collective-permute-start.4) | collective-permute-done | bytes 589856 | tf_op jit(solution)/shard_map/ppermute | solution.py:60
  89.0 4.1 %collective-permute-done.13.refs_8_ = bf16[4,96,768]{2,1,0:T(8,128)(2,1)} collective-permute-done((bf16[4,96,768]{2,1,0:T(8,128)(2,1)}, bf16[4,96,768]{2,1,0:T(8,128)(2,1)}, u32[]{:S(2)}, u32[]{:S(2)}) %collective-permute-start.13) | collective-permute-done | bytes 589856 | tf_op jit(solution)/shard_map/ppermute | solution.py:60
  100.5 20.8 %attention_forward.1 = (bf16[512,768]{1,0:T(8,128)(2,1)}, bf16[6,512,128]{2,1,0:T(8,128)(2,1)}, bf16[6,512,128]{2,1,0:T(8,128)(2,1)}, bf16[6,512,128]{2,1,0:T(8,...) custom-call(s32[32]{0:T(128)} %get-tuple-element.114.refs_0_, ...), custom_call_target="tpu_custom_call" | custom-call | flops 3019898880 | bytes 13653152 | tf_op jit(solution)/shard_map/attention_forward/pallas_call | solution.py:238
  121.4 16.9 %mlp_forward.1 = (bf16[4,512,768]{2,1,0:T(8,128)(2,1)}, bf16[4,512,768]{2,1,0:T(8,128)(2,1)}, bf16[16,96,768]{2,1,0:T(8,128)(2,1)}, bf16[16,96,768]{2,1,0:T(8,128)(2,1)}) custom-call(s32[32]{0:T(128)} %get-tuple-element.114.refs_0_, s32[4]{0:T(128)} %pad_add_fusion.refs_1_, bf16[512,768]{1,0:T(8,128)(2,1)} %get-tuple-element.57.refs_2_.refs_4_, ...), custom_call_target="tpu_custom_call" | custom-call | flops 4831838208 | bytes 17313936 | tf_op jit(solution)/shard_map/mlp_forward/pallas_call | solution.py:238
  139.7 14.9 %mlp_backward.1 = (bf16[4,512,768]{2,1,0:T(8,128)(2,1)}, f32[4,1,768]{2,1,0:T(1,128)}, bf16[16,96,768]{2,1,0:T(8,128)(2,1)}, bf16[16,96,768]{2,1,0:T(8,128)(2,1)}) custom-call(s32[32]{0:T(128)} %get-tuple-element.114.refs_0_, s32[4]{0:T(128)} %pad_add_fusion.refs_1_, bf16[512,768]{1,0:T(8,128)(2,1)} %broadcast_select_fusion.refs_3_.refs_2_, ...), custom_call_target="tpu_custom_call" | custom-call | flops 4831838208 | bytes 17313936 | tf_op jit(solution)/shard_map/mlp_backward/pallas_call | solution.py:238
  154.6 10.0 %middle_backward.1 = (f32[512,768]{1,0:T(8,128)}, bf16[512,768]{1,0:T(8,128)(2,1)}, f32[4,768]{1,0:T(4,128)}) custom-call(s32[32]{0:T(128)} %get-tuple-element.114.refs_0_, bf16[4,512,768]{2,1,0:T(8,128)(2,1)} %get-tuple-element.61.refs_1_, f32[512,768]{1,0:T(8,128)} %get-tuple-element.59.refs_2_, bf16[512,768]{1,0:T(8,128)(2,1)} %broadcast_select_fusion.refs_3_.refs_2_, ...), custom_call_target="tpu_custom_call" | custom-call | flops 2415919104 | bytes 12607616 | tf_op jit(solution)/shard_map/middle_backward/pallas_call | solution.py:238
  164.6 22.0 %attention_backward.1 = (bf16[4,512,640]{2,1,0:T(8,128)(2,1)}, f32[6,128]{1,0:T(8,128)}, f32[6,128]{1,0:T(8,128)}, bf16[16,96,768]{2,1,0:T(8,128)(2,1)}, bf16[16,96,768]{2,1,0:T(8,128)(2,1)}) custom-call(s32[32]{0:T(128)} %get-tuple-element.114.refs_0_, s32[4]{0:T(128)} %pad_add_fusion.refs_1_, bf16[512,768]{1,0:T(8,128)(2,1)} %get-tuple-element.62.refs_2_, ...), custom_call_target="tpu_custom_call" | custom-call | flops 4227858432 | bytes 18618512 | tf_op jit(solution)/shard_map/attention_backward/pallas_call | solution.py:238
  191.1 9.6 %input_backward.1 = (f32[512,768]{1,0:T(8,128)}, f32[2,768]{1,0:T(2,128)}) custom-call(s32[32]{0:T(128)} %get-tuple-element.114.refs_0_, bf16[4,512,640]{2,1,0:T(8,128)(2,1)} %get-tuple-element.69.refs_1_, bf16[512,768]{1,0:T(8,128)(2,1)} %refs_2_.3, f32[512,768]{1,0:T(8,128)} %get-tuple-element.70.refs_3_, f32[4,768]{1,0:T(4,128)} %refs_4_.3, ...), custom_call_target="tpu_custom_call" | custom-call | flops 1811939328 | bytes 11290752 | tf_op jit(solution)/shard_map/input_backward/pallas_call | solution.py:238
  205.5 3.0 collective-permute-done.43
  213.7 2.7 add_convert_fusion.1
  219.9 8.6 %block_out.1 = bf16[512,768]{1,0:T(8,128)(2,1)} custom-call(s32[32]{0:T(128)} %get-tuple-element.114.refs_0_, bf16[4,512,768]{2,1,0:T(8,128)(2,1)} %get-tuple-element.58.refs_1_, f32[512,768]{1,0:T(8,128)} %get-tuple-element.59.refs_2_, f32[1,768]{1,0:T(1,128)} %get-tuple-element.128.refs_3_, bf16[4,96,768]{2,1,0:T(8,128)(2,1)} %copy-done, ...), custom_call_target="tpu_custom_call" | custom-call | flops 2415919104 | bytes 10226816 | tf_op jit(solution)/shard_map/block_out/pallas_call | solution.py:238
  228.5 2.7 collective-permute-start.46
  235.0 13.1 %collective-permute-done.33 = bf16[8,96,768]{2,1,0:T(8,128)(2,1)} collective-permute-done((bf16[8,96,768]{2,1,0:T(8,128)(2,1)}, bf16[8,96,768]{2,1,0:T(8,128)(2,1)}, u32[]{:S(2)}, u32[]{:S(2)}) %collective-permute-start.33) | collective-permute-done | bytes 1179680 | tf_op jit(solution)/shard_map/ppermute | solution.py:60
  250.3 16.6 %collective-permute-done.38 = bf16[8,96,768]{2,1,0:T(8,128)(2,1)} collective-permute-done((bf16[8,96,768]{2,1,0:T(8,128)(2,1)}, bf16[8,96,768]{2,1,0:T(8,128)(2,1)}, u32[]{:S(2)}, u32[]{:S(2)}) %collective-permute-start.38) | collective-permute-done | bytes 1179680 | tf_op jit(solution)/shard_map/ppermute | solution.py:60
  271.7 3.0 collective-permute-start.35
  274.6 3.4 collective-permute-done.39
  279.5 15.9 %collective-permute-done.30 = bf16[2,96,768]{2,1,0:T(8,128)(2,1)S(1)} collective-permute-done((bf16[2,96,768]{2,1,0:T(8,128)(2,1)S(1)}, bf16[2,96,768]{2,1,0:T(8,128)(2,1)S(1)}, u32[]{:S(2)}, u32[]{:S(2)}) %collective-permute-start.30) | collective-permute-done | bytes 294944 | tf_op jit(solution)/shard_map/ppermute | solution.py:60
  295.6 6.2 %collective-permute-done.35 = bf16[2,96,768]{2,1,0:T(8,128)(2,1)S(1)} collective-permute-done((bf16[2,96,768]{2,1,0:T(8,128)(2,1)S(1)}, bf16[2,96,768]{2,1,0:T(8,128)(2,1)S(1)}, u32[]{:S(2)}, u32[]{:S(2)}) %collective-permute-start.35) | collective-permute-done | bytes 294944 | tf_op jit(solution)/shard_map/ppermute | solution.py:60
  301.9 4.2 %collective-permute-done.40 = bf16[2,96,768]{2,1,0:T(8,128)(2,1)S(1)} collective-permute-done((bf16[2,96,768]{2,1,0:T(8,128)(2,1)S(1)}, bf16[2,96,768]{2,1,0:T(8,128)(2,1)S(1)}, u32[]{:S(2)}, u32[]{:S(2)}) %collective-permute-start.40) | collective-permute-done | bytes 294944 | tf_op jit(solution)/shard_map/ppermute | solution.py:60
  306.3 3.0 collective-permute-done.31
  333.3 3.1 collective-permute-done.51
  (286 shorter events, 82.4 us)
Async XLA Ops:
  9.8 15.5 %collective-permute-start.1 = (bf16[2,96,768]{2,1,0:T(8,128)(2,1)S(1)}, bf16[2,96,768]{2,1,0:T(8,128)(2,1)S(1)}, u32[]{:S(2)}, u32[]{:S(2)}) collective-permute-start(bf16[2,96,768]{2,1,0:T(8,128)(2,1)S(1)} %pad_maximum_fusion.3), channel_id=1, source_target_pairs={{0,16},{1,17},{2,18},{3,19},{4,20},{5,21},{6,22},{7,23},{8,24},{9,... | collective-permute-start | bytes 884744 | tf_op jit(solution)/shard_map/ppermute | solution.py:60
  12.7 16.4 %collective-permute-start.9 = (bf16[1,96,768]{2,1,0:T(8,128)(2,1)S(1)}, bf16[1,96,768]{2,1,0:T(8,128)(2,1)S(1)}, u32[]{:S(2)}, u32[]{:S(2)}) collective-permute-start(bf16[1,96,768]{2,1,0:T(8,128)(2,1)S(1)} %convert_bitcast_fusion.1), channel_id=1, source_target_pairs={{0,8},{1,9},{2,10},{3,11},{4,12},{5,13},{6,14},{7,15},{8,0},{9,1},... | collective-permute-start | bytes 442376 | tf_op jit(solution)/shard_map/ppermute | solution.py:60
  25.4 33.0 %collective-permute-start.2 = (bf16[4,96,768]{2,1,0:T(8,128)(2,1)S(1)}, bf16[4,96,768]{2,1,0:T(8,128)(2,1)}, u32[]{:S(2)}, u32[]{:S(2)}) collective-permute-start(bf16[4,96,768]{2,1,0:T(8,128)(2,1)S(1)} %pad_maximum_fusion.refs_7_.refs_9_.refs_5_), channel_id=1, source_target_pairs={{0,4},{1,3},{2,6},{3,1},{4,0},{5,7},{6,2},{7,5},{8,12},{9,11},{10,... | collective-permute-start | bytes 1769480 | tf_op jit(solution)/shard_map/ppermute | solution.py:60
  27.5 30.9 %collective-permute-start.3 = (bf16[4,96,768]{2,1,0:T(8,128)(2,1)S(1)}, bf16[4,96,768]{2,1,0:T(8,128)(2,1)}, u32[]{:S(2)}, u32[]{:S(2)}) collective-permute-start(bf16[4,96,768]{2,1,0:T(8,128)(2,1)S(1)} %pad_maximum_fusion.refs_7_.refs_9_.refs_5_), channel_id=1, source_target_pairs={{0,2},{1,5},{2,0},{3,7},{4,6},{5,1},{6,4},{7,3},{8,10},{9,13},{10,... | collective-permute-start | bytes 1769480 | tf_op jit(solution)/shard_map/ppermute | solution.py:60
  29.1 23.6 %collective-permute-start.10 = (bf16[2,96,768]{2,1,0:T(8,128)(2,1)S(1)}, bf16[2,96,768]{2,1,0:T(8,128)(2,1)S(1)}, u32[]{:S(2)}, u32[]{:S(2)}) collective-permute-start(bf16[2,96,768]{2,1,0:T(8,128)(2,1)S(1)} %pad_maximum_fusion.4), channel_id=1, source_target_pairs={{0,16},{1,17},{2,18},{3,19},{4,20},{5,21},{6,22},{7,23},{8,24},{9,... | collective-permute-start | bytes 884744 | tf_op jit(solution)/shard_map/ppermute | solution.py:60
  32.7 25.2 %collective-permute-start.19 = (bf16[2,96,768]{2,1,0:T(8,128)(2,1)S(1)}, bf16[2,96,768]{2,1,0:T(8,128)(2,1)S(1)}, u32[]{:S(2)}, u32[]{:S(2)}) collective-permute-start(bf16[2,96,768]{2,1,0:T(8,128)(2,1)S(1)} %pad_maximum_fusion.5), channel_id=1, source_target_pairs={{0,16},{1,17},{2,18},{3,19},{4,20},{5,21},{6,22},{7,23},{8,24},{9,... | collective-permute-start | bytes 884744 | tf_op jit(solution)/shard_map/ppermute | solution.py:60
  35.8 23.3 %collective-permute-start.5 = (bf16[4,96,768]{2,1,0:T(8,128)(2,1)S(1)}, bf16[4,96,768]{2,1,0:T(8,128)(2,1)S(1)}, u32[]{:S(2)}, u32[]{:S(2)}) collective-permute-start(bf16[4,96,768]{2,1,0:T(8,128)(2,1)S(1)} %pad_maximum_fusion.refs_7_.refs_9_.refs_5_), channel_id=1, source_target_pairs={{0,1},{1,0},{2,3},{3,2},{4,5},{5,4},{6,7},{7,6},{8,9},{9,8},{10,11... | collective-permute-start | bytes 1769480 | tf_op jit(solution)/shard_map/ppermute | solution.py:60
  57.8 16.0 %collective-permute-start.12 = (bf16[4,96,768]{2,1,0:T(8,128)(2,1)S(1)}, bf16[4,96,768]{2,1,0:T(8,128)(2,1)S(1)}, u32[]{:S(2)}, u32[]{:S(2)}) collective-permute-start(bf16[4,96,768]{2,1,0:T(8,128)(2,1)S(1)} %pad_maximum_fusion.1.refs_5_), channel_id=1, source_target_pairs={{0,2},{1,5},{2,0},{3,7},{4,6},{5,1},{6,4},{7,3},{8,10},{9,13},{10,... | collective-permute-start | bytes 1769480 | tf_op jit(solution)/shard_map/ppermute | solution.py:60
  58.3 15.5 %collective-permute-start.14 = (bf16[4,96,768]{2,1,0:T(8,128)(2,1)S(1)}, bf16[4,96,768]{2,1,0:T(8,128)(2,1)S(1)}, u32[]{:S(2)}, u32[]{:S(2)}) collective-permute-start(bf16[4,96,768]{2,1,0:T(8,128)(2,1)S(1)} %pad_maximum_fusion.1.refs_5_), channel_id=1, source_target_pairs={{0,1},{1,0},{2,3},{3,2},{4,5},{5,4},{6,7},{7,6},{8,9},{9,8},{10,11... | collective-permute-start | bytes 1769480 | tf_op jit(solution)/shard_map/ppermute | solution.py:60
  58.4 20.1 %collective-permute-start.20 = (bf16[4,96,768]{2,1,0:T(8,128)(2,1)S(1)}, bf16[4,96,768]{2,1,0:T(8,128)(2,1)S(1)}, u32[]{:S(2)}, u32[]{:S(2)}) collective-permute-start(bf16[4,96,768]{2,1,0:T(8,128)(2,1)S(1)} %pad_maximum_fusion.2.refs_4_.refs_5_), channel_id=1, source_target_pairs={{0,4},{1,3},{2,6},{3,1},{4,0},{5,7},{6,2},{7,5},{8,12},{9,11},{10,... | collective-permute-start | bytes 1769480 | tf_op jit(solution)/shard_map/ppermute | solution.py:60
  59.1 21.7 %collective-permute-start.21 = (bf16[4,96,768]{2,1,0:T(8,128)(2,1)S(1)}, bf16[4,96,768]{2,1,0:T(8,128)(2,1)S(1)}, u32[]{:S(2)}, u32[]{:S(2)}) collective-permute-start(bf16[4,96,768]{2,1,0:T(8,128)(2,1)S(1)} %pad_maximum_fusion.2.refs_4_.refs_5_), channel_id=1, source_target_pairs={{0,2},{1,5},{2,0},{3,7},{4,6},{5,1},{6,4},{7,3},{8,10},{9,13},{10,... | collective-permute-start | bytes 1769480 | tf_op jit(solution)/shard_map/ppermute | solution.py:60
  66.0 20.8 %collective-permute-start.4 = (bf16[4,96,768]{2,1,0:T(8,128)(2,1)}, bf16[4,96,768]{2,1,0:T(8,128)(2,1)}, u32[]{:S(2)}, u32[]{:S(2)}) collective-permute-start(bf16[4,96,768]{2,1,0:T(8,128)(2,1)} %collective-permute-done.2.refs_8_.refs_10_.refs_6_), channel_id=1, source_target_pairs={{0,2},{1,5},{2,0},{3,7},{4,6},{5,1},{6,4},{7,3},{8,10},{9,13},{10,... | collective-permute-start | bytes 1769480 | tf_op jit(solution)/shard_map/ppermute | solution.py:60
  73.9 14.3 %collective-permute-start.6 = (bf16[4,96,768]{2,1,0:T(8,128)(2,1)}, bf16[4,96,768]{2,1,0:T(8,128)(2,1)}, u32[]{:S(2)}, u32[]{:S(2)}) collective-permute-start(bf16[4,96,768]{2,1,0:T(8,128)(2,1)} %collective-permute-done.2.refs_8_.refs_10_.refs_6_), channel_id=1, source_target_pairs={{0,1},{1,0},{2,3},{3,2},{4,5},{5,4},{6,7},{7,6},{8,9},{9,8},{10,11... | collective-permute-start | bytes 1769480 | tf_op jit(solution)/shard_map/ppermute | solution.py:60
  78.6 14.6 %collective-permute-start.13 = (bf16[4,96,768]{2,1,0:T(8,128)(2,1)}, bf16[4,96,768]{2,1,0:T(8,128)(2,1)}, u32[]{:S(2)}, u32[]{:S(2)}) collective-permute-start(bf16[4,96,768]{2,1,0:T(8,128)(2,1)} %collective-permute-done.11.refs_6_), channel_id=1, source_target_pairs={{0,2},{1,5},{2,0},{3,7},{4,6},{5,1},{6,4},{7,3},{8,10},{9,13},{10,... | collective-permute-start | bytes 1769480 | tf_op jit(solution)/shard_map/ppermute | solution.py:60
  80.8 16.1 %collective-permute-start.15 = (bf16[4,96,768]{2,1,0:T(8,128)(2,1)}, bf16[4,96,768]{2,1,0:T(8,128)(2,1)}, u32[]{:S(2)}, u32[]{:S(2)}) collective-permute-start(bf16[4,96,768]{2,1,0:T(8,128)(2,1)} %collective-permute-done.11.refs_6_), channel_id=1, source_target_pairs={{0,1},{1,0},{2,3},{3,2},{4,5},{5,4},{6,7},{7,6},{8,9},{9,8},{10,11... | collective-permute-start | bytes 1769480 | tf_op jit(solution)/shard_map/ppermute | solution.py:60
  93.1 28.3 %collective-permute-start.17 = (bf16[4,96,768]{2,1,0:T(8,128)(2,1)}, bf16[4,96,768]{2,1,0:T(8,128)(2,1)}, u32[]{:S(2)}, u32[]{:S(2)}) collective-permute-start(bf16[4,96,768]{2,1,0:T(8,128)(2,1)} %collective-permute-done.13.refs_8_), channel_id=1, source_target_pairs={{0,1},{1,0},{2,3},{3,2},{4,5},{5,4},{6,7},{7,6},{8,9},{9,8},{10,11... | collective-permute-start | bytes 1769480 | tf_op jit(solution)/shard_map/ppermute | solution.py:60
  96.9 41.4 %collective-permute-start.23 = (bf16[4,96,768]{2,1,0:T(8,128)(2,1)S(1)}, bf16[4,96,768]{2,1,0:T(8,128)(2,1)S(1)}, u32[]{:S(2)}, u32[]{:S(2)}) collective-permute-start(bf16[4,96,768]{2,1,0:T(8,128)(2,1)S(1)} %pad_maximum_fusion.2.refs_4_.refs_5_), channel_id=1, source_target_pairs={{0,1},{1,0},{2,3},{3,2},{4,5},{5,4},{6,7},{7,6},{8,9},{9,8},{10,11... | collective-permute-start | bytes 1769480 | tf_op jit(solution)/shard_map/ppermute | solution.py:60
  96.9 41.4 %collective-permute-start.24 = (bf16[4,96,768]{2,1,0:T(8,128)(2,1)S(1)}, bf16[4,96,768]{2,1,0:T(8,128)(2,1)S(1)}, u32[]{:S(2)}, u32[]{:S(2)}) collective-permute-start(bf16[4,96,768]{2,1,0:T(8,128)(2,1)S(1)} %collective-permute-done.20.refs_5_.refs_6_), channel_id=1, source_target_pairs={{0,1},{1,0},{2,3},{3,2},{4,5},{5,4},{6,7},{7,6},{8,9},{9,8},{10,11... | collective-permute-start | bytes 1769480 | tf_op jit(solution)/shard_map/ppermute | solution.py:60
  99.4 38.9 %collective-permute-start.25 = (bf16[4,96,768]{2,1,0:T(8,128)(2,1)S(1)}, bf16[4,96,768]{2,1,0:T(8,128)(2,1)S(1)}, u32[]{:S(2)}, u32[]{:S(2)}) collective-permute-start(bf16[4,96,768]{2,1,0:T(8,128)(2,1)S(1)} %collective-permute-done.21.refs_6_.refs_7_), channel_id=1, source_target_pairs={{0,1},{1,0},{2,3},{3,2},{4,5},{5,4},{6,7},{7,6},{8,9},{9,8},{10,11... | collective-permute-start | bytes 1769480 | tf_op jit(solution)/shard_map/ppermute | solution.py:60
  100.5 37.8 %collective-permute-start.26 = (bf16[4,96,768]{2,1,0:T(8,128)(2,1)}, bf16[4,96,768]{2,1,0:T(8,128)(2,1)S(1)}, u32[]{:S(2)}, u32[]{:S(2)}) collective-permute-start(bf16[4,96,768]{2,1,0:T(8,128)(2,1)} %collective-permute-done.22.refs_7_.refs_8_), channel_id=1, source_target_pairs={{0,1},{1,0},{2,3},{3,2},{4,5},{5,4},{6,7},{7,6},{8,9},{9,8},{10,11... | collective-permute-start | bytes 1769480 | tf_op jit(solution)/shard_map/ppermute | solution.py:60
  186.6 22.9 %collective-permute-start.27 = (bf16[16,96,768]{2,1,0:T(8,128)(2,1)}, bf16[16,96,768]{2,1,0:T(8,128)(2,1)}, u32[]{:S(2)}, u32[]{:S(2)}) collective-permute-start(bf16[16,96,768]{2,1,0:T(8,128)(2,1)} %get-tuple-element.73), channel_id=1, source_target_pairs={{0,1},{1,0},{2,3},{3,2},{4,5},{5,4},{6,7},{7,6},{8,9},{9,8},{10,11... | collective-permute-start | bytes 7077896 | tf_op jit(solution)/shard_map/ppermute | solution.py:60
  187.8 25.8 %collective-permute-start.32 = (bf16[16,96,768]{2,1,0:T(8,128)(2,1)}, bf16[16,96,768]{2,1,0:T(8,128)(2,1)}, u32[]{:S(2)}, u32[]{:S(2)}) collective-permute-start(bf16[16,96,768]{2,1,0:T(8,128)(2,1)} %get-tuple-element.75), channel_id=1, source_target_pairs={{0,1},{1,0},{2,3},{3,2},{4,5},{5,4},{6,7},{7,6},{8,9},{9,8},{10,11... | collective-permute-start | bytes 7077896 | tf_op jit(solution)/shard_map/ppermute | solution.py:60
  187.9 29.3 %collective-permute-start.37 = (bf16[16,96,768]{2,1,0:T(8,128)(2,1)}, bf16[16,96,768]{2,1,0:T(8,128)(2,1)S(1)}, u32[]{:S(2)}, u32[]{:S(2)}) collective-permute-start(bf16[16,96,768]{2,1,0:T(8,128)(2,1)} %get-tuple-element.77), channel_id=1, source_target_pairs={{0,1},{1,0},{2,3},{3,2},{4,5},{5,4},{6,7},{7,6},{8,9},{9,8},{10,11... | collective-permute-start | bytes 7077896 | tf_op jit(solution)/shard_map/ppermute | solution.py:60
  211.5 19.6 %collective-permute-start.28 = (bf16[8,96,768]{2,1,0:T(8,128)(2,1)S(1)}, bf16[8,96,768]{2,1,0:T(8,128)(2,1)}, u32[]{:S(2)}, u32[]{:S(2)}) collective-permute-start(bf16[8,96,768]{2,1,0:T(8,128)(2,1)S(1)} %add_convert_fusion.2), channel_id=1, source_target_pairs={{0,2},{1,5},{2,0},{3,7},{4,6},{5,1},{6,4},{7,3},{8,10},{9,13},{10,... | collective-permute-start | bytes 3538952 | tf_op jit(solution)/shard_map/ppermute | solution.py:60
  213.6 14.9 %collective-permute-start.45 = (f32[2,288]{1,0:T(2,128)S(1)}, f32[2,288]{1,0:T(2,128)S(1)}, u32[]{:S(2)}, u32[]{:S(2)}) collective-permute-start(f32[2,288]{1,0:T(2,128)S(1)} %slice.406), channel_id=1, source_target_pairs={{0,16},{1,17},{2,18},{3,19},{4,20},{5,21},{6,22},{7,23},{8,24},{9,... | collective-permute-start | bytes 6920 | tf_op jit(solution)/shard_map/ppermute | solution.py:60
  216.4 31.7 %collective-permute-start.33 = (bf16[8,96,768]{2,1,0:T(8,128)(2,1)}, bf16[8,96,768]{2,1,0:T(8,128)(2,1)}, u32[]{:S(2)}, u32[]{:S(2)}) collective-permute-start(bf16[8,96,768]{2,1,0:T(8,128)(2,1)} %add_convert_fusion.1), channel_id=1, source_target_pairs={{0,2},{1,5},{2,0},{3,7},{4,6},{5,1},{6,4},{7,3},{8,10},{9,13},{10,... | collective-permute-start | bytes 3538952 | tf_op jit(solution)/shard_map/ppermute | solution.py:60
  218.6 48.2 %collective-permute-start.38 = (bf16[8,96,768]{2,1,0:T(8,128)(2,1)}, bf16[8,96,768]{2,1,0:T(8,128)(2,1)}, u32[]{:S(2)}, u32[]{:S(2)}) collective-permute-start(bf16[8,96,768]{2,1,0:T(8,128)(2,1)} %add_convert_fusion), channel_id=1, source_target_pairs={{0,2},{1,5},{2,0},{3,7},{4,6},{5,1},{6,4},{7,3},{8,10},{9,13},{10,... | collective-permute-start | bytes 3538952 | tf_op jit(solution)/shard_map/ppermute | solution.py:60
  232.8 35.4 %collective-permute-start.29 = (bf16[4,96,768]{2,1,0:T(8,128)(2,1)S(1)}, bf16[4,96,768]{2,1,0:T(8,128)(2,1)S(1)}, u32[]{:S(2)}, u32[]{:S(2)}) collective-permute-start(bf16[4,96,768]{2,1,0:T(8,128)(2,1)S(1)} %add_convert_fusion.5), channel_id=1, source_target_pairs={{0,4},{1,3},{2,6},{3,1},{4,0},{5,7},{6,2},{7,5},{8,12},{9,11},{10,... | collective-permute-start | bytes 1769480 | tf_op jit(solution)/shard_map/ppermute | solution.py:60
  249.6 20.5 %collective-permute-start.34 = (bf16[4,96,768]{2,1,0:T(8,128)(2,1)S(1)}, bf16[4,96,768]{2,1,0:T(8,128)(2,1)S(1)}, u32[]{:S(2)}, u32[]{:S(2)}) collective-permute-start(bf16[4,96,768]{2,1,0:T(8,128)(2,1)S(1)} %add_convert_fusion.4), channel_id=1, source_target_pairs={{0,4},{1,3},{2,6},{3,1},{4,0},{5,7},{6,2},{7,5},{8,12},{9,11},{10,... | collective-permute-start | bytes 1769480 | tf_op jit(solution)/shard_map/ppermute | solution.py:60
  270.0 25.4 %collective-permute-start.30 = (bf16[2,96,768]{2,1,0:T(8,128)(2,1)S(1)}, bf16[2,96,768]{2,1,0:T(8,128)(2,1)S(1)}, u32[]{:S(2)}, u32[]{:S(2)}) collective-permute-start(bf16[2,96,768]{2,1,0:T(8,128)(2,1)S(1)} %slice.494), channel_id=1, source_target_pairs={{0,16},{1,17},{2,18},{3,19},{4,20},{5,21},{6,22},{7,23},{8,24},{9,... | collective-permute-start | bytes 884744 | tf_op jit(solution)/shard_map/ppermute | solution.py:60
  271.7 30.1 %collective-permute-start.35 = (bf16[2,96,768]{2,1,0:T(8,128)(2,1)S(1)}, bf16[2,96,768]{2,1,0:T(8,128)(2,1)S(1)}, u32[]{:S(2)}, u32[]{:S(2)}) collective-permute-start(bf16[2,96,768]{2,1,0:T(8,128)(2,1)S(1)} %slice.493), channel_id=1, source_target_pairs={{0,16},{1,17},{2,18},{3,19},{4,20},{5,21},{6,22},{7,23},{8,24},{9,... | collective-permute-start | bytes 884744 | tf_op jit(solution)/shard_map/ppermute | solution.py:60
  279.4 26.7 %collective-permute-start.40 = (bf16[2,96,768]{2,1,0:T(8,128)(2,1)S(1)}, bf16[2,96,768]{2,1,0:T(8,128)(2,1)S(1)}, u32[]{:S(2)}, u32[]{:S(2)}) collective-permute-start(bf16[2,96,768]{2,1,0:T(8,128)(2,1)S(1)} %slice.492), channel_id=1, source_target_pairs={{0,16},{1,17},{2,18},{3,19},{4,20},{5,21},{6,22},{7,23},{8,24},{9,... | collective-permute-start | bytes 884744 | tf_op jit(solution)/shard_map/ppermute | solution.py:60
  (69 other events, 1252.9 us)
